TPU v7x, 32 devices: a whole 2x2x4 slice. The times are simulated.
32 devices in a mesh: space: 16 (over z, y, core), dom: 2 (over x).
Axes of the slice: x: 2, y: 2, z: 4, core: 2. Of those that a mesh axis runs over, the one named last changes fastest.
Arguments:
- water_depth: float32 [4, 16, 256, 512], P('dom', 'space'), may hold values from 0 to 1.5
- infiltrated: float32 [4, 16, 256, 512], P('dom', 'space'), may hold values from 0.2 to 2
- terrain: float32 [16, 256, 512], P('space'), may hold values from -3 to 3
- land_mask: int32 [16, 256, 512], P('space'), may hold values from 0 to 1
- forcing: bfloat16 [2, 2, 16, 256, 512], P(None, None, 'space', 'dom'), may hold values from 0.049804688 to 1.5
- observed: bfloat16 [2, 16, 256, 512], P(None, 'space'), may hold values from 0 to 3.6
- conductivity: float32 [4], replicated, may hold values from 0.05 to 0.6
- suction: float32 [4], replicated, may hold values from 0.1 to 2
- manning: float32 [4], replicated, may hold values from 0.5 to 2
- assignment: int32 [4], P('dom'), may hold values from 0 to 3, each once
- ancestors: int32 [4], P('dom'), may hold values from 0 to 3, as said below
- prior_weight: float32 [4], P('dom'), may hold values from 0.01 to 1
Outputs:
- final_depth: float32 [4, 16, 256, 512], P('dom', 'space')
- final_infiltrated: float32 [4, 16, 256, 512], P('dom', 'space')
- weights: float32 [4], P('dom')
Inputs may be any that keep to these rules, and one draw needn't show every extreme that they name: `ancestors`: the ancestor of slot s is a slot of its own group, 2 * (s // 2) to 2 * (s // 2) + 1; slot 0's ancestor is 0 and the last slot's is itself.
All inputs are finite; a program needn't handle non-finite values.
Results may differ from a plain program's by a relative error of at most 0.0003.
Values may be sent and summed in bfloat16 or wider, within the bound.
A program may use at most 64 MiB of HBM per device.

v0:
```python
import jax
import jax.numpy as jnp
from jax import lax
from jax.sharding import PartitionSpec as P

TX = 4
SUB = 6
HOURS = 2


time_step = 0.01
slope_floor = 0.1
sharpness = 20.0


def passed_along(block, axis, distance):
    devices = range(lax.axis_size(axis))
    route = [(i - distance, i) for i in devices if i - distance in devices]
    return lax.ppermute(block, axis, route)


def passed_along_2(array, axis, by):
    devices = lax.axis_size(axis)
    return lax.ppermute(array, axis, [(i, (i + by) % devices) for i in range(devices)])


def deep_row_shift(edge, offset):
    return passed_along(edge.astype(jnp.bfloat16), "space", offset).astype(edge.dtype)


def deep_col_shift(edge, offset):
    return passed_along_2(edge, "space", offset)


def from_west(edge, column_tile, shifter):
    near = shifter(edge, 1)
    far = shifter(edge, -(TX - 1))
    return jnp.where(column_tile == 0, far, near)


def from_east(edge, column_tile, shifter):
    near = shifter(edge, -1)
    far = shifter(edge, TX - 1)
    return jnp.where(column_tile == TX - 1, far, near)


def deep_rims(field, width, column_tile):
    west = from_west(field[..., :, -width:], column_tile, deep_col_shift)
    east = from_east(field[..., :, :width], column_tile, deep_col_shift)
    wide = jnp.concatenate([west, field, east], axis=-1)
    north = deep_row_shift(wide[..., -width:, :], TX)
    south = deep_row_shift(wide[..., :width, :], -TX)
    return jnp.concatenate([north, wide, south], axis=-2)


def face_flux(depth_a, depth_b, level_a, level_b, rough):
    slope = level_b - level_a
    mean_depth = 0.5 * (depth_a + depth_b)
    return (
        -jnp.power(mean_depth, 5.0 / 3.0) * slope / (rough * jnp.sqrt(jnp.abs(slope) + slope_floor))
    )


def flow_step(depth_now, soak_now, padded, level, net_rain, land, conduct, suction_p, rough):
    flux_cols = face_flux(
        padded[:, 1:-1, :-1], padded[:, 1:-1, 1:], level[:, 1:-1, :-1], level[:, 1:-1, 1:], rough
    )
    flux_rows = face_flux(
        padded[:, :-1, 1:-1], padded[:, 1:, 1:-1], level[:, :-1, 1:-1], level[:, 1:, 1:-1], rough
    )
    outflow = (
        flux_cols[:, :, 1:] - flux_cols[:, :, :-1] + flux_rows[:, 1:, :] - flux_rows[:, :-1, :]
    )
    ponded = jnp.maximum(depth_now - time_step * outflow + time_step * net_rain, 0.0)
    capacity = conduct * (1.0 + suction_p / soak_now)
    intake = jnp.minimum(time_step * capacity, ponded)
    return ((ponded - intake) * land, soak_now + intake * land)


def local(
    water_depth,
    infiltrated,
    terrain,
    land_mask,
    forcing,
    observed,
    conductivity,
    suction,
    manning,
    assignment,
    ancestors,
    prior_weight,
):
    per_group = water_depth.shape[0]
    first_slot = lax.axis_index("dom") * per_group
    local_slot = ancestors - first_slot
    water = jnp.take(water_depth[:, 0], local_slot, axis=0)
    soaked = jnp.take(infiltrated[:, 0], local_slot, axis=0)
    owners = jnp.take(assignment, local_slot)
    every_slot = jnp.arange(conductivity.shape[0], dtype=jnp.int32)
    picker = owners[:, None] == every_slot[None, :]

    def lookup(table):
        return jnp.sum(jnp.where(picker, table[None, :], 0.0), axis=1)[:, None, None]

    conduct = lookup(conductivity)
    suction_p = lookup(suction)
    rough = lookup(manning)
    group_mean = jnp.mean(prior_weight)
    column_tile = lax.axis_index("space") % TX
    land = land_mask[0].astype(jnp.float32)
    width = SUB
    static_big = deep_rims(jnp.stack([terrain[0], land], axis=0), width, column_tile)
    ground_big = jnp.pad(static_big[0], 1)
    land_big = static_big[1]
    window_forcing = lax.all_gather(forcing, "dom", axis=3, tiled=True)
    misfit = jnp.zeros((per_group,), jnp.float32)
    for hour in range(HOURS):
        hour_forcing = window_forcing[hour]
        net_rain = hour_forcing[0, 0].astype(jnp.float32) - hour_forcing[1, 0].astype(jnp.float32)
        stacked = jnp.concatenate([water, soaked, net_rain[None]], axis=0)
        big = deep_rims(stacked, width, column_tile)
        depth_big = big[:per_group]
        soak_big = big[per_group : 2 * per_group]
        soak_big = jnp.where(soak_big > 0.0, soak_big, 1.0)
        rain_big = big[2 * per_group]

        def advance_big(index, carry):
            depth_now, soak_now = carry
            padded = jnp.pad(depth_now, ((0, 0), (1, 1), (1, 1)))
            level = padded + ground_big[None]
            return flow_step(
                depth_now, soak_now, padded, level, rain_big, land_big, conduct, suction_p, rough
            )

        depth_big, soak_big = lax.fori_loop(0, SUB, advance_big, (depth_big, soak_big))
        water = depth_big[:, width:-width, width:-width]
        soaked = soak_big[:, width:-width, width:-width]
        gap = water - observed[hour, 0].astype(jnp.float32)
        square = gap * gap
        misfit = misfit + jnp.sum(land * square / (1.0 + square), axis=(1, 2))
    cells = HOURS * jnp.sum(land)
    summed = lax.psum((misfit, cells), "space")
    raw = group_mean * jnp.exp(-sharpness * summed[0] / summed[1])
    total = lax.psum(jnp.sum(raw), "dom")
    weights = raw / total
    return (water[:, None], soaked[:, None], weights)


def solution(mesh):
    return jax.shard_map(
        local,
        mesh=mesh,
        in_specs=(
            P("dom", "space", None, None),
            P("dom", "space", None, None),
            P("space", None, None),
            P("space", None, None),
            P(None, None, "space", "dom", None),
            P(None, "space", None, None),
            P(),
            P(),
            P(),
            P("dom"),
            P("dom"),
            P("dom"),
        ),
        out_specs=(P("dom", "space", None, None), P("dom", "space", None, None), P("dom")),
        check_vma=False,
    )
```

profile of v0, /device:TPU:0, one launch (start us, length us, event | category | flops | bytes accessed | tf_op | source)
XLA Modules:
  0.0 289.9 jit_solution(5018392547327523656)
XLA Ops:
  7.2 2.0 convert_bitcast_fusion
  10.2 4.5 %collective-permute-start.6 = (f32[2,256,6]{2,1,0:T(8,128)}, f32[2,256,6]{2,1,0:T(8,128)}, u32[]{:S(2)}, u32[]{:S(2)}) collective-permute-start(f32[2,256,6]{2,1,0:T(8,128)} %get-tuple-element.331), channel_id=1, source_target_pairs={{0,26},{2,28},{4,30},{6,0},{8,2},{10,4},{12,6},{14,8},{16,10},{18,... | collective-permute-start | bytes 36872 | tf_op jit(solution)/shard_map/ppermute | solution.py:24
  14.7 1.6 collective-permute-start.7
  16.3 2.9 collective-permute-start.9
  22.4 2.8 broadcast_select_fusion.1
  30.0 3.4 %collective-permute-start.10 = (bf16[2,6,524]{2,1,0:T(8,128)(2,1)S(1)}, bf16[2,6,524]{2,1,0:T(8,128)(2,1)S(1)}, u32[]{:S(2)}, u32[]{:S(2)}) collective-permute-start(bf16[2,6,524]{2,1,0:T(8,128)(2,1)S(1)} %get-tuple-element.326), channel_id=1, source_target_pairs={{0,8},{2,10},{4,12},{6,14},{8,16},{10,18},{12,20},{14,22},{16,24},... | collective-permute-start | bytes 37736 | tf_op jit(solution)/shard_map/ppermute | solution.py:19
  35.0 4.1 %collective-permute-done.11 = bf16[2,6,524]{2,1,0:T(8,128)(2,1)S(1)} collective-permute-done((bf16[2,6,524]{2,1,0:T(8,128)(2,1)S(1)}, bf16[2,6,524]{2,1,0:T(8,128)(2,1)S(1)}, u32[]{:S(2)}, u32[]{:S(2)}) %collective-permute-start.11) | collective-permute-done | bytes 12608 | tf_op jit(solution)/shard_map/ppermute | solution.py:19
  39.5 2.1 subtract_bitcast_fusion.1
  41.6 2.3 pad_maximum_fusion.8
  45.2 2.8 collective-permute-start
  49.6 2.8 pad_maximum_fusion.2
  53.8 2.9 %collective-permute-start.3 = (f32[5,256,6]{1,2,0:T(8,128)S(1)}, f32[5,256,6]{1,2,0:T(8,128)S(1)}, u32[]{:S(2)}, u32[]{:S(2)}) collective-permute-start(f32[5,256,6]{1,2,0:T(8,128)S(1)} %copy.50), channel_id=1, source_target_pairs={{0,30},{2,0},{4,2},{6,4},{8,6},{10,8},{12,10},{14,12},{16,14},{18,... | collective-permute-start | bytes 92168 | tf_op jit(solution)/shard_map/ppermute | solution.py:24
  68.5 3.3 %collective-permute-done.5 = bf16[5,6,524]{2,1,0:T(8,128)(2,1)S(1)} collective-permute-done((bf16[5,6,524]{2,1,0:T(8,128)(2,1)S(1)}, bf16[5,6,524]{2,1,0:T(8,128)(2,1)S(1)}, u32[]{:S(2)}, u32[]{:S(2)}) %collective-permute-start.5) | collective-permute-done | bytes 31472 | tf_op jit(solution)/shard_map/ppermute | solution.py:19
  73.0 2.6 pad_maximum_fusion
  76.9 56.5 %while.28 = (s32[]{:T(128)}, f32[2,268,524]{2,1,0:T(8,128)S(1)}, f32[2,268,524]{2,1,0:T(8,128)}, f32[270,526]{1,0:T(8,128)}, f32[2,1,1]{0,2,1:T(1,128)S(1)}, /*i...) while((s32[]{:T(128)}, f32[2,268,524]{2,1,0:T(8,128)S(1)}, ...), condition=%wide.region_4.6_spmd, body=%wide.region_3.5_spmd.sunk | while | flops 11392426 | bytes 35988860 | solution.py:136
  76.9 1.6 pad_add_fusion.4
  78.5 1.9 multiply_divide_fusion.8
  80.4 1.9 multiply_divide_fusion.9
  86.3 1.6 pad_add_fusion.4
  87.9 1.9 multiply_divide_fusion.8
  89.8 1.9 multiply_divide_fusion.9
  95.7 1.6 pad_add_fusion.4
  97.3 1.9 multiply_divide_fusion.8
  99.3 1.9 multiply_divide_fusion.9
  105.1 1.6 pad_add_fusion.4
  106.7 1.9 multiply_divide_fusion.8
  108.7 1.9 multiply_divide_fusion.9
  114.5 1.6 pad_add_fusion.4
  116.1 1.9 multiply_divide_fusion.8
  118.1 1.9 multiply_divide_fusion.9
  124.0 1.6 pad_add_fusion.4
  125.6 1.9 multiply_divide_fusion.8
  127.5 1.9 multiply_divide_fusion.9
  138.5 2.1 collective-permute-start.13
  140.6 2.1 bitcast_convert_fusion.1
  144.1 2.5 collective-permute-start.15
  148.8 2.0 broadcast_select_fusion.4
  160.8 2.3 collective-permute-done.17
  163.1 2.5 maximum_bitcast_fusion
  165.6 2.6 pad_maximum_fusion.1
  168.3 1.7 compare_select_fusion
  170.0 65.8 %while.29 = (s32[]{:T(128)}, f32[2,268,524]{2,1,0:T(8,128)}, f32[2,268,524]{2,1,0:T(8,128)}, f32[270,526]{1,0:T(8,128)}, f32[2,1,1]{0,2,1:T(1,128)S(1)}, /*index...) while((s32[]{:T(128)}, f32[2,268,524]{2,1,0:T(8,128)}, ...), condition=%wide.region_6.8_spmd, body=%wide.region_5.7_spmd.sunk | while | flops 11392426 | bytes 40482712 | solution.py:136
  170.0 2.1 pad_add_fusion.5
  172.1 1.9 multiply_divide_fusion.10
  174.1 1.9 multiply_divide_fusion.11
  181.0 2.1 pad_add_fusion.5
  183.1 1.9 multiply_divide_fusion.10
  185.0 1.9 multiply_divide_fusion.11
  191.9 2.1 pad_add_fusion.5
  194.1 1.9 multiply_divide_fusion.10
  196.0 1.9 multiply_divide_fusion.11
  202.9 2.1 pad_add_fusion.5
  205.0 1.9 multiply_divide_fusion.10
  207.0 1.9 multiply_divide_fusion.11
  213.9 2.1 pad_add_fusion.5
  216.0 1.9 multiply_divide_fusion.10
  217.9 1.9 multiply_divide_fusion.11
  224.8 2.1 pad_add_fusion.5
  227.0 1.9 multiply_divide_fusion.10
  228.9 1.9 multiply_divide_fusion.11
  235.8 3.6 %fusion.9 = (f32[2]{0:T(128)S(1)}, f32[2]{0:T(128)S(1)}, f32[2,1,256,512]{3,2,1,0:T(8,128)}) fusion(f32[2,268,524]{2,1,0:T(8,128)} %get-tuple-element.234, f32[256,512]{1,0:T(8,128)} %get-tuple-element.336, f32[256,512]{1,0:T(8,128)} %get-tuple-element.337, f32[256,512]{1,0:T(8,128)} %get-tuple-element.335, f32[2,268,524]{2,1,0:T(8,128)S(1)} %get-tuple-element.232), kind=kLoop, calls=%fused_computation.44 | loop fusion | flops 3145724 | bytes 4718608 | tf_op jit(solution)/shard_map/reduce_sum | solution.py:141
  240.1 32.3 %all-reduce.3 = (f32[2]{0:T(128)S(1)}, f32[]{:T(128)}) all-reduce(f32[2]{0:T(128)S(1)} %add.190, f32[]{:T(128)S(6)} %mul.298), channel_id=1, replica_groups=mesh['space'=16,'dom'=2] {'space'}, use_global_device_ids=true, to_apply=%region_10.12 | all-reduce | flops 3 | bytes 24 | tf_op jit(solution)/shard_map/psum | solution.py:143
  273.7 5.6 %psum.23 = f32[]{:T(128)} all-reduce(f32[]{:T(128)} %get-tuple-element.310), channel_id=1, replica_groups=mesh['space'=16,'dom'=2] {'dom'}, use_global_device_ids=true, to_apply=%region_14.16 | all-reduce | flops 1 | bytes 8 | tf_op jit(solution)/shard_map/psum | solution.py:145
  279.3 2.6 slice_bitcast_fusion
  (238 shorter events, 102.3 us)
Async XLA Ops:
  7.2 12.1 %copy-start = (f32[2,1,256,512]{3,2,1,0:T(8,128)S(1)}, f32[2,1,256,512]{3,2,1,0:T(8,128)}, u32[]{:S(2)}) copy-start(f32[2,1,256,512]{3,2,1,0:T(8,128)} %param.18) | copy-start | bytes 3145732
  7.2 2.1 copy-start.23
  7.2 32.3 %all-gather.2.cloned.1.call-start = ((), (), s32[]{:S(2)}) async-start(), calls=%async_computation | async-start | bytes 1572864 | tf_op jit(solution)/shard_map/all_gather | solution.py:116
  9.3 9.9 %copy-start.31 = (s32[2]{0:T(128)S(1)}, s32[2]{0:T(128)}, u32[]{:S(2)}) copy-start(s32[2]{0:T(128)} %param.28) | copy-start | bytes 28
  10.2 10.7 %copy-start.27 = (f32[2,1,256,512]{3,2,1,0:T(8,128)S(1)}, f32[2,1,256,512]{3,2,1,0:T(8,128)}, u32[]{:S(2)}) copy-start(f32[2,1,256,512]{3,2,1,0:T(8,128)} %param.19) | copy-start | bytes 3145732
  10.2 15.7 %collective-permute-start.6 = (f32[2,256,6]{2,1,0:T(8,128)}, f32[2,256,6]{2,1,0:T(8,128)}, u32[]{:S(2)}, u32[]{:S(2)}) collective-permute-start(f32[2,256,6]{2,1,0:T(8,128)} %get-tuple-element.331), channel_id=1, source_target_pairs={{0,26},{2,28},{4,30},{6,0},{8,2},{10,4},{12,6},{14,8},{16,10},{18,... | collective-permute-start | bytes 36872 | tf_op jit(solution)/shard_map/ppermute | solution.py:24
  14.7 11.2 %collective-permute-start.7 = (f32[2,256,6]{2,1,0:T(8,128)}, f32[2,256,6]{2,1,0:T(8,128)}, u32[]{:S(2)}, u32[]{:S(2)}) collective-permute-start(f32[2,256,6]{2,1,0:T(8,128)} %get-tuple-element.331), channel_id=1, source_target_pairs={{0,2},{2,4},{4,6},{6,8},{8,10},{10,12},{12,14},{14,16},{16,18},{18... | collective-permute-start | bytes 36872 | tf_op jit(solution)/shard_map/ppermute | solution.py:24
  16.3 12.0 %collective-permute-start.8 = (f32[2,256,6]{2,1,0:T(8,128)}, f32[2,256,6]{2,1,0:T(8,128)}, u32[]{:S(2)}, u32[]{:S(2)}) collective-permute-start(f32[2,256,6]{2,1,0:T(8,128)} %get-tuple-element.332), channel_id=1, source_target_pairs={{0,6},{2,8},{4,10},{6,12},{8,14},{10,16},{12,18},{14,20},{16,22},{... | collective-permute-start | bytes 36872 | tf_op jit(solution)/shard_map/ppermute | solution.py:24
  16.3 12.0 %collective-permute-start.9 = (f32[2,256,6]{2,1,0:T(8,128)}, f32[2,256,6]{2,1,0:T(8,128)}, u32[]{:S(2)}, u32[]{:S(2)}) collective-permute-start(f32[2,256,6]{2,1,0:T(8,128)} %get-tuple-element.332), channel_id=1, source_target_pairs={{0,30},{2,0},{4,2},{6,4},{8,6},{10,8},{12,10},{14,12},{16,14},{18,... | collective-permute-start | bytes 36872 | tf_op jit(solution)/shard_map/ppermute | solution.py:24
  22.4 2.8 copy-start.2
  26.9 2.5 copy-start.24
  26.9 7.8 %copy-start.28 = (f32[4]{0:T(128)S(1)}, f32[4]{0:T(128)}, u32[]{:S(2)}) copy-start(f32[4]{0:T(128)} %param.25) | copy-start | bytes 52
  26.9 7.8 %copy-start.29 = (f32[4]{0:T(128)S(1)}, f32[4]{0:T(128)}, u32[]{:S(2)}) copy-start(f32[4]{0:T(128)} %param.24) | copy-start | bytes 52
  26.9 7.8 %copy-start.30 = (f32[4]{0:T(128)S(1)}, f32[4]{0:T(128)}, u32[]{:S(2)}) copy-start(f32[4]{0:T(128)} %param.26) | copy-start | bytes 52
  30.0 5.0 %collective-permute-start.10 = (bf16[2,6,524]{2,1,0:T(8,128)(2,1)S(1)}, bf16[2,6,524]{2,1,0:T(8,128)(2,1)S(1)}, u32[]{:S(2)}, u32[]{:S(2)}) collective-permute-start(bf16[2,6,524]{2,1,0:T(8,128)(2,1)S(1)} %get-tuple-element.326), channel_id=1, source_target_pairs={{0,8},{2,10},{4,12},{6,14},{8,16},{10,18},{12,20},{14,22},{16,24},... | collective-permute-start | bytes 37736 | tf_op jit(solution)/shard_map/ppermute | solution.py:19
  33.4 5.7 %collective-permute-start.11 = (bf16[2,6,524]{2,1,0:T(8,128)(2,1)S(1)}, bf16[2,6,524]{2,1,0:T(8,128)(2,1)S(1)}, u32[]{:S(2)}, u32[]{:S(2)}) collective-permute-start(bf16[2,6,524]{2,1,0:T(8,128)(2,1)S(1)} %get-tuple-element.327), channel_id=1, source_target_pairs={{8,0},{10,2},{12,4},{14,6},{16,8},{18,10},{20,12},{22,14},{24,16},... | collective-permute-start | bytes 37736 | tf_op jit(solution)/shard_map/ppermute | solution.py:19
  45.2 11.5 %collective-permute-start = (f32[5,256,6]{1,2,0:T(8,128)S(1)}, f32[5,256,6]{1,2,0:T(8,128)S(1)}, u32[]{:S(2)}, u32[]{:S(2)}) collective-permute-start(f32[5,256,6]{1,2,0:T(8,128)S(1)} %copy.46), channel_id=1, source_target_pairs={{0,26},{2,28},{4,30},{6,0},{8,2},{10,4},{12,6},{14,8},{16,10},{18,... | collective-permute-start | bytes 92168 | tf_op jit(solution)/shard_map/ppermute | solution.py:24
  48.0 9.8 %collective-permute-start.1 = (f32[5,256,6]{1,2,0:T(8,128)S(1)}, f32[5,256,6]{1,2,0:T(8,128)S(1)}, u32[]{:S(2)}, u32[]{:S(2)}) collective-permute-start(f32[5,256,6]{1,2,0:T(8,128)S(1)} %copy.46), channel_id=1, source_target_pairs={{0,2},{2,4},{4,6},{6,8},{8,10},{10,12},{12,14},{14,16},{16,18},{18... | collective-permute-start | bytes 92168 | tf_op jit(solution)/shard_map/ppermute | solution.py:24
  53.7 6.3 %collective-permute-start.2 = (f32[5,256,6]{1,2,0:T(8,128)S(1)}, f32[5,256,6]{1,2,0:T(8,128)S(1)}, u32[]{:S(2)}, u32[]{:S(2)}) collective-permute-start(f32[5,256,6]{1,2,0:T(8,128)S(1)} %copy.50), channel_id=1, source_target_pairs={{0,6},{2,8},{4,10},{6,12},{8,14},{10,16},{12,18},{14,20},{16,22},{... | collective-permute-start | bytes 92168 | tf_op jit(solution)/shard_map/ppermute | solution.py:24
  53.8 7.4 %collective-permute-start.3 = (f32[5,256,6]{1,2,0:T(8,128)S(1)}, f32[5,256,6]{1,2,0:T(8,128)S(1)}, u32[]{:S(2)}, u32[]{:S(2)}) collective-permute-start(f32[5,256,6]{1,2,0:T(8,128)S(1)} %copy.50), channel_id=1, source_target_pairs={{0,30},{2,0},{4,2},{6,4},{8,6},{10,8},{12,10},{14,12},{16,14},{18,... | collective-permute-start | bytes 92168 | tf_op jit(solution)/shard_map/ppermute | solution.py:24
  60.1 3.4 %copy-start.18 = (f32[5,256,6]{2,1,0:T(8,128)}, f32[5,256,6]{2,1,0:T(8,128)S(1)}, u32[]{:S(2)}) copy-start(f32[5,256,6]{2,1,0:T(8,128)S(1)} %broadcast_select_fusion.5) | copy-start | bytes 92164
  63.5 3.8 %copy-start.22 = (f32[2,268,524]{2,1,0:T(8,128)S(1)}, f32[2,268,524]{2,1,0:T(8,128)}, u32[]{:S(2)}) copy-start(f32[2,268,524]{2,1,0:T(8,128)} %pad_maximum_fusion.2) | copy-start | bytes 3370372
  64.5 4.0 %collective-permute-start.4 = (bf16[5,6,524]{2,1,0:T(8,128)(2,1)S(1)}, bf16[5,6,524]{2,1,0:T(8,128)(2,1)S(1)}, u32[]{:S(2)}, u32[]{:S(2)}) collective-permute-start(bf16[5,6,524]{2,1,0:T(8,128)(2,1)S(1)} %get-tuple-element.316), channel_id=1, source_target_pairs={{0,8},{2,10},{4,12},{6,14},{8,16},{10,18},{12,20},{14,22},{16,24},... | collective-permute-start | bytes 94328 | tf_op jit(solution)/shard_map/ppermute | solution.py:19
  65.8 6.0 %collective-permute-start.5 = (bf16[5,6,524]{2,1,0:T(8,128)(2,1)S(1)}, bf16[5,6,524]{2,1,0:T(8,128)(2,1)S(1)}, u32[]{:S(2)}, u32[]{:S(2)}) collective-permute-start(bf16[5,6,524]{2,1,0:T(8,128)(2,1)S(1)} %get-tuple-element.317), channel_id=1, source_target_pairs={{8,0},{10,2},{12,4},{14,6},{16,8},{18,10},{20,12},{22,14},{24,16},... | collective-permute-start | bytes 94328 | tf_op jit(solution)/shard_map/ppermute | solution.py:19
  67.3 4.5 %copy-start.19 = (f32[5,256,6]{2,1,0:T(8,128)S(1)}, f32[5,256,6]{2,1,0:T(8,128)}, u32[]{:S(2)}) copy-start(f32[5,256,6]{2,1,0:T(8,128)} %copy-done.18) | copy-start | bytes 92164
  67.4 4.4 %copy-start.6 = (f32[2,256,512]{2,1,0:T(8,128)S(1)}, f32[2,256,512]{2,1,0:T(8,128)}, u32[]{:S(2)}) copy-start(f32[2,256,512]{2,1,0:T(8,128)} %get-tuple-element.340) | copy-start | bytes 3145732
  80.4 2.0 copy-start.13
  89.8 2.0 copy-start.13
  91.8 1.3 copy-start.3
  99.3 2.0 copy-start.13
  108.7 2.0 copy-start.13
  118.1 2.0 copy-start.13
  127.5 2.0 copy-start.13
  133.4 1.5 copy-start.4
  133.7 2.9 %copy-start.7 = (f32[2,256,512]{2,1,0:T(8,128)}, f32[2,256,512]{2,1,0:T(8,128)S(1)}, u32[]{:S(2)}) copy-start(f32[2,256,512]{2,1,0:T(8,128)S(1)} %slice.265) | copy-start | bytes 3145732
  133.7 1.5 copy-start.14
  135.2 1.4 copy-start.10
  138.0 8.6 %collective-permute-start.12 = (f32[5,256,6]{1,2,0:T(8,128)S(1)}, f32[5,256,6]{1,2,0:T(8,128)S(1)}, u32[]{:S(2)}, u32[]{:S(2)}) collective-permute-start(f32[5,256,6]{1,2,0:T(8,128)S(1)} %copy.54), channel_id=1, source_target_pairs={{0,26},{2,28},{4,30},{6,0},{8,2},{10,4},{12,6},{14,8},{16,10},{18,... | collective-permute-start | bytes 92168 | tf_op jit(solution)/shard_map/ppermute | solution.py:24
  138.5 9.2 %collective-permute-start.13 = (f32[5,256,6]{1,2,0:T(8,128)S(1)}, f32[5,256,6]{1,2,0:T(8,128)S(1)}, u32[]{:S(2)}, u32[]{:S(2)}) collective-permute-start(f32[5,256,6]{1,2,0:T(8,128)S(1)} %copy.54), channel_id=1, source_target_pairs={{0,2},{2,4},{4,6},{6,8},{8,10},{10,12},{12,14},{14,16},{16,18},{18... | collective-permute-start | bytes 92168 | tf_op jit(solution)/shard_map/ppermute | solution.py:24
  144.0 6.8 %collective-permute-start.14 = (f32[5,256,6]{1,2,0:T(8,128)S(1)}, f32[5,256,6]{1,2,0:T(8,128)S(1)}, u32[]{:S(2)}, u32[]{:S(2)}) collective-permute-start(f32[5,256,6]{1,2,0:T(8,128)S(1)} %copy.58), channel_id=1, source_target_pairs={{0,6},{2,8},{4,10},{6,12},{8,14},{10,16},{12,18},{14,20},{16,22},{... | collective-permute-start | bytes 92168 | tf_op jit(solution)/shard_map/ppermute | solution.py:24
  144.1 7.8 %collective-permute-start.15 = (f32[5,256,6]{1,2,0:T(8,128)S(1)}, f32[5,256,6]{1,2,0:T(8,128)S(1)}, u32[]{:S(2)}, u32[]{:S(2)}) collective-permute-start(f32[5,256,6]{1,2,0:T(8,128)S(1)} %copy.58), channel_id=1, source_target_pairs={{0,30},{2,0},{4,2},{6,4},{8,6},{10,8},{12,10},{14,12},{16,14},{18,... | collective-permute-start | bytes 92168 | tf_op jit(solution)/shard_map/ppermute | solution.py:24
  153.1 1.4 copy-start.8
  153.1 1.6 copy-start.15
  154.6 4.0 %copy-start.26 = (s32[1,256,512]{2,1,0:T(8,128)S(1)}, s32[1,256,512]{2,1,0:T(8,128)}, u32[]{:S(2)}) copy-start(s32[1,256,512]{2,1,0:T(8,128)} %param.21) | copy-start | bytes 1572868
  154.6 4.8 %copy-start.32 = (f32[2]{0:T(128)S(1)}, f32[2]{0:T(128)}, u32[]{:S(2)}) copy-start(f32[2]{0:T(128)} %param.29) | copy-start | bytes 28
  155.8 5.0 %collective-permute-start.16 = (bf16[5,6,524]{2,1,0:T(8,128)(2,1)S(1)}, bf16[5,6,524]{2,1,0:T(8,128)(2,1)S(1)}, u32[]{:S(2)}, u32[]{:S(2)}) collective-permute-start(bf16[5,6,524]{2,1,0:T(8,128)(2,1)S(1)} %get-tuple-element.314), channel_id=1, source_target_pairs={{0,8},{2,10},{4,12},{6,14},{8,16},{10,18},{12,20},{14,22},{16,24},... | collective-permute-start | bytes 94328 | tf_op jit(solution)/shard_map/ppermute | solution.py:19
  157.1 6.0 %collective-permute-start.17 = (bf16[5,6,524]{2,1,0:T(8,128)(2,1)S(1)}, bf16[5,6,524]{2,1,0:T(8,128)(2,1)S(1)}, u32[]{:S(2)}, u32[]{:S(2)}) collective-permute-start(bf16[5,6,524]{2,1,0:T(8,128)(2,1)S(1)} %get-tuple-element.315), channel_id=1, source_target_pairs={{8,0},{10,2},{12,4},{14,6},{16,8},{18,10},{20,12},{22,14},{24,16},... | collective-permute-start | bytes 94328 | tf_op jit(solution)/shard_map/ppermute | solution.py:19
  163.1 2.5 copy-start.9
  163.1 2.5 copy-start.11
  163.1 2.5 copy-start.16
  163.1 2.5 copy-start.17
  163.1 2.5 copy-start.21
  170.0 2.1 copy-start.1
  174.1 2.0 copy-start.12
  180.9 2.1 copy-start.1
  185.0 2.0 copy-start.12
  191.9 2.1 copy-start.1
  196.0 2.0 copy-start.12
  202.9 2.1 copy-start.1
  207.0 2.0 copy-start.12
  213.9 2.1 copy-start.1
  217.9 2.0 copy-start.12
  224.8 2.1 copy-start.1
  228.9 2.0 copy-start.12
  (13 other events, 16.7 us)
Sparse Core Ops, SparseCore 0:
  19.3 20.1 all-gather.1
where the time goes:
time: 292 us; the launch traced here: 290 us
  other arithmetic  139 us (48%)
  local copies, waits for them, and re-layouts  53.3 us (18%)
  blocking collectives  38 us (13%)
  starting transfers between devices  31.8 us (11%)
  between operations  15.9 us (5%)
  waiting for transfers between devices  11.5 us (4%)
    div x24, other arithmetic, face_flux(): -jnp.power(mean_depth, 5.0 / 3.0) * slope  46.5 us
    psum x1, blocking collectives, local(): summed = lax.psum((misfit, cells), 'space')  32.3 us
    while x72, local copies, waits for them, and re-layouts  28.6 us
    add x12, other arithmetic, advance_big(): level = padded + ground_big[None]  22.2 us
    ppermute x12, starting transfers between devices, passed_along_2(): lax.ppermute(array, axis, [(i, (i + by) % devices) for i in range(devices)])  21.5 us
    mul x12, other arithmetic, flow_step(): return ((ponded - intake) * land, soak_now + intake * land)  12.5 us
    add x12, other arithmetic, flow_step(): return ((ponded - intake) * land, soak_now + intake * land)  10.9 us
    ppermute x6, starting transfers between devices, passed_along(): return lax.ppermute(block, axis, route)  10.3 us
  transfers between devices with their start and end apart: 19, of which 5 were waited for; matrix products, arithmetic and copies ran while one was open for 10% of the time, Pallas kernels for 0%

commit v1 on v0

v1 whole, which is shorter than its diff:
```python
import functools
import math

import jax
import jax.numpy as jnp
from jax import lax
from jax.experimental import pallas as pl
from jax.experimental.pallas import tpu as pltpu
from jax.sharding import PartitionSpec as P

TX = 4
SUB = 6
MESH = pl.DeviceIdType.MESH

time_step = 0.01
slope_floor = 0.1
sharpness = 20.0
DRY = -1e30
LANES = 128
ROWS = 8


def passed_along(block, axis, distance):
    devices = range(lax.axis_size(axis))
    route = [(i - distance, i) for i in devices if i - distance in devices]
    return lax.ppermute(block, axis, route)


def passed_along_2(array, axis, by):
    devices = lax.axis_size(axis)
    return lax.ppermute(array, axis, [(i, (i + by) % devices) for i in range(devices)])


def from_west(edge, column_tile):
    near = passed_along_2(edge, "space", 1)
    far = passed_along_2(edge, "space", -(TX - 1))
    return jnp.where(column_tile == 0, far, near)


def from_east(edge, column_tile):
    near = passed_along_2(edge, "space", -1)
    far = passed_along_2(edge, "space", TX - 1)
    return jnp.where(column_tile == TX - 1, far, near)


def face(depth_sum, slope):
    power = jnp.exp2(jnp.log(depth_sum) * (5.0 / 3.0 / math.log(2.0)))
    return power * slope * lax.rsqrt(jnp.abs(slope) + slope_floor)


def window_kernel(
    hours, width, rim, par_ref, d_in, s_in, g_ref, r_ref, obs_ref,
    depth_out, soak_out, miss_out, d_ref, s_ref, ge_ref, gs_ref,
):
    parts, high, wide = d_in.shape
    own_rows, own_cols = depth_out.shape[1:]
    cols = wide // LANES
    blocks = high // ROWS
    top = rim // ROWS
    bottom = top + own_rows // ROWS
    lane = lax.broadcasted_iota(jnp.int32, (ROWS, LANES), 1)
    sub = lax.broadcasted_iota(jnp.int32, (ROWS, LANES), 0)
    first_lane, last_lane = lane == 0, lane == LANES - 1
    first_sub, last_sub = sub == 0, sub == ROWS - 1

    def at(block, j):
        return pl.ds(pl.multiple_of(block * ROWS, ROWS), ROWS), pl.ds(j * LANES, LANES)

    def east(here, beside):
        return pltpu.roll(jnp.where(first_lane, beside, here), LANES - 1, 1)

    def south(here, below):
        return pltpu.roll(jnp.where(first_sub, below, here), ROWS - 1, 0)

    def prepare(block, carry):
        below = jnp.minimum(block + 1, blocks - 1)
        for j in range(cols):
            here = g_ref[at(block, j)]
            ge_ref[at(block, j)] = east(here, g_ref[at(block, (j + 1) % cols)]) - here
            gs_ref[at(block, j)] = south(here, g_ref[at(below, j)]) - here
            for p in range(parts):
                d_ref[(p,) + at(block, j)] = d_in[(p,) + at(block, j)]
                s_ref[(p,) + at(block, j)] = s_in[(p,) + at(block, j)]
        return carry

    lax.fori_loop(0, blocks, prepare, 0)
    for p in range(parts):
        d_ref[p, pl.ds(high, ROWS), :] = jnp.zeros((ROWS, wide), jnp.float32)

    for hour in range(hours):

        def substep(index, carry):
            left = hours * SUB - 1 - (hour * SUB + index)
            start = top - 1 - left // ROWS
            stop = bottom + (left + ROWS - 1) // ROWS

            def step(block, above):
                out = []
                for p in range(parts):
                    k, a, b = par_ref[0, p], par_ref[1, p], par_ref[2, p]
                    d = [d_ref[(p,) + at(block, j)] for j in range(cols)]

                    def col_face(j):
                        d_e = east(d[j], d[(j + 1) % cols])
                        return face(d[j] + d_e, (d_e - d[j]) + ge_ref[at(block, j)])

                    last = col_face(cols - 1)
                    west = last
                    for j in range(cols):
                        f_e = last if j == cols - 1 else col_face(j)
                        f_w = pltpu.roll(jnp.where(last_lane, west, f_e), 1, 1)
                        west = f_e
                        d_s = south(d[j], d_ref[(p,) + at(block + 1, j)])
                        f_s = face(d[j] + d_s, (d_s - d[j]) + gs_ref[at(block, j)])
                        f_n = pltpu.roll(jnp.where(last_sub, above[p * cols + j], f_s), 1, 0)
                        out.append(f_s)
                        gain = (f_e - f_w) + (f_s - f_n)
                        ponded = jnp.maximum(d[j] + k * gain + r_ref[(hour,) + at(block, j)], 0.0)
                        soak = s_ref[(p,) + at(block, j)]
                        inverse = pl.reciprocal(soak, approx=True)
                        inverse = inverse * (2.0 - soak * inverse)
                        intake = jnp.minimum(a + b * inverse, ponded)
                        d_ref[(p,) + at(block, j)] = ponded - intake
                        s_ref[(p,) + at(block, j)] = soak + intake
                return tuple(out)

            zero = jnp.zeros((ROWS, LANES), jnp.float32)
            lax.fori_loop(start, stop, step, (zero,) * (parts * cols))
            return carry

        lax.fori_loop(0, SUB, substep, 0)

        def score(block, sums):
            sums = list(sums)
            for j in range(own_cols // LANES):
                seen = obs_ref[(hour,) + at(block, j)]
                for p in range(parts):
                    gap = d_ref[(p,) + at(block + top, j)] - seen
                    square = gap * gap
                    sums[p] += jnp.where(seen >= 0.0, square / (1.0 + square), 0.0)
            return tuple(sums)

        zero = jnp.zeros((ROWS, LANES), jnp.float32)
        sums = lax.fori_loop(0, own_rows // ROWS, score, (zero,) * parts)
        for p in range(parts):
            miss_out[p] = sums[p] if hour == 0 else miss_out[p] + sums[p]

    def finish(block, carry):
        for j in range(own_cols // LANES):
            for p in range(parts):
                depth_out[(p,) + at(block, j)] = d_ref[(p,) + at(block + top, j)]
                soak_out[(p,) + at(block, j)] = s_ref[(p,) + at(block + top, j)]
        return carry

    lax.fori_loop(0, own_rows // ROWS, finish, 0)


def weigh_kernel(n_space, n_dom, parts, mine_ref, out_ref, held, send_sem, recv_sem):
    total = n_space * n_dom
    space, dom = lax.axis_index("space"), lax.axis_index("dom")
    me = space * n_dom + dom
    barrier = pltpu.get_barrier_semaphore()

    def place(i):
        other = lax.rem(me + i, total)
        return (other // n_dom, lax.rem(other, n_dom))

    def greet(i, carry):
        pl.semaphore_signal(barrier, inc=1, device_id=place(i), device_id_type=MESH)
        return carry

    lax.fori_loop(1, total, greet, 0)
    pl.semaphore_wait(barrier, total - 1)

    def copy(i):
        return pltpu.make_async_remote_copy(
            src_ref=mine_ref, dst_ref=held.at[i], send_sem=send_sem.at[i], recv_sem=recv_sem.at[i],
            device_id=place(i), device_id_type=MESH,
        )

    def send(i, carry):
        copy(i).start()
        return carry

    def arrive(i, carry):
        copy(i).wait()
        return carry

    lax.fori_loop(1, total, send, 0)
    held[0] = mine_ref[...]
    lax.fori_loop(1, total, arrive, 0)

    def add(i, sums):
        theirs = lax.rem(lax.rem(me - i + total, total), n_dom)
        block = held[i]
        return tuple(s + jnp.where(theirs == g, block, 0.0) for g, s in enumerate(sums))

    zero = jnp.zeros(mine_ref.shape, jnp.float32)
    sums = lax.fori_loop(0, total, add, (zero,) * n_dom)
    whole = jnp.zeros((1, 1), jnp.float32)
    own = zero[0:1]
    lane = lax.broadcasted_iota(jnp.int32, (1, LANES), 1)
    for g in range(n_dom):
        misfit, cells, mean = sums[g][0:1], sums[g][1:2], sums[g][2:3] / n_space
        raw = jnp.where(lane < parts, mean * jnp.exp(-sharpness * misfit / cells), 0.0)
        whole = whole + jnp.sum(raw, axis=1, keepdims=True)
        own = jnp.where(dom == g, raw, own)
    out_ref[...] = jnp.broadcast_to(own / whole, out_ref.shape)


def local(
    n_space, n_dom,
    water_depth, infiltrated, terrain, land_mask, forcing, observed,
    conductivity, suction, manning, assignment, ancestors, prior_weight,
):
    parts, _, rows, columns = water_depth.shape
    hours = observed.shape[0]
    width = hours * SUB
    rim = -(-width // ROWS) * ROWS
    first_slot = lax.axis_index("dom") * parts
    local_slot = ancestors - first_slot
    water = jnp.take(water_depth[:, 0], local_slot, axis=0)
    soaked = jnp.take(infiltrated[:, 0], local_slot, axis=0)
    owners = jnp.take(assignment, local_slot)
    every_slot = jnp.arange(conductivity.shape[0], dtype=jnp.int32)
    picker = owners[:, None] == every_slot[None, :]

    def lookup(table):
        return jnp.sum(jnp.where(picker, table[None, :], 0.0), axis=1)

    conduct, suction_p, rough = lookup(conductivity), lookup(suction), lookup(manning)
    params = jnp.stack(
        [time_step * 0.5 ** (5.0 / 3.0) / rough, time_step * conduct, time_step * conduct * suction_p]
    )
    group_mean = jnp.mean(prior_weight)
    column_tile = lax.axis_index("space") % TX
    row_tile = lax.axis_index("space") // TX
    land = land_mask[0] > 0
    forced = lax.all_gather(forcing, "dom", axis=3, tiled=True)[:, :, 0].astype(jnp.float32)
    rain = jnp.where(land[None], time_step * (forced[:, 0] - forced[:, 1]), DRY)
    fields = jnp.concatenate([water, soaked, terrain, rain], axis=0)
    fill = jnp.array([0.0] * parts + [1.0] * parts + [0.0] + [DRY] * hours, jnp.float32)[:, None, None]
    west = from_west(fields[:, :, -width:], column_tile)
    east = from_east(fields[:, :, :width], column_tile)
    gap = jnp.broadcast_to(fill, (fields.shape[0], rows, LANES - 2 * width))
    wide = jnp.concatenate([fields, east, gap, west], axis=-1)
    north = passed_along(wide[:, -rim:, :], "space", TX)
    south = passed_along(wide[:, :rim, :], "space", -TX)
    north = jnp.where(row_tile == 0, fill, north)
    south = jnp.where(row_tile == n_space // TX - 1, fill, south)
    big = jnp.concatenate([north, wide, south], axis=-2)
    high, across = big.shape[1:]
    seen = jnp.where(land[None], observed[:, 0].astype(jnp.float32), -1.0)
    vmem = pl.BlockSpec(memory_space=pltpu.VMEM)
    depth, soak, missed = pl.pallas_call(
        functools.partial(window_kernel, hours, width, rim),
        out_shape=(
            jax.ShapeDtypeStruct((parts, rows, columns), jnp.float32),
            jax.ShapeDtypeStruct((parts, rows, columns), jnp.float32),
            jax.ShapeDtypeStruct((parts, ROWS, LANES), jnp.float32),
        ),
        in_specs=[pl.BlockSpec(memory_space=pltpu.SMEM)] + [vmem] * 5,
        out_specs=(vmem, vmem, vmem),
        scratch_shapes=[
            pltpu.VMEM((parts, high + ROWS, across), jnp.float32),
            pltpu.VMEM((parts, high, across), jnp.float32),
            pltpu.VMEM((high, across), jnp.float32),
            pltpu.VMEM((high, across), jnp.float32),
        ],
        compiler_params=pltpu.CompilerParams(vmem_limit_bytes=48 * 2**20),
    )(params, big[:parts], big[parts : 2 * parts], big[2 * parts], big[2 * parts + 1 :], seen)
    misfit = jnp.sum(missed, axis=(1, 2))
    cells = hours * jnp.sum(land.astype(jnp.float32))
    mine = jnp.zeros((ROWS, LANES), jnp.float32).at[0, :parts].set(misfit).at[1].set(cells).at[2].set(group_mean)
    total = n_space * n_dom
    weights = pl.pallas_call(
        functools.partial(weigh_kernel, n_space, n_dom, parts),
        out_shape=jax.ShapeDtypeStruct((ROWS, LANES), jnp.float32),
        in_specs=[vmem],
        out_specs=vmem,
        scratch_shapes=[
            pltpu.VMEM((total, ROWS, LANES), jnp.float32),
            pltpu.SemaphoreType.DMA((total,)),
            pltpu.SemaphoreType.DMA((total,)),
        ],
        compiler_params=pltpu.CompilerParams(collective_id=0, has_side_effects=True),
    )(mine)
    return depth[:, None], soak[:, None], weights[0, :parts]


def solution(mesh):
    return jax.shard_map(
        functools.partial(local, mesh.shape["space"], mesh.shape["dom"]),
        mesh=mesh,
        in_specs=(
            P("dom", "space", None, None),
            P("dom", "space", None, None),
            P("space", None, None),
            P("space", None, None),
            P(None, None, "space", "dom", None),
            P(None, "space", None, None),
            P(),
            P(),
            P(),
            P("dom"),
            P("dom"),
            P("dom"),
        ),
        out_specs=(P("dom", "space", None, None), P("dom", "space", None, None), P("dom")),
        check_vma=False,
    )
```

time: 292 us -> 284 us (0.973)
  Pallas kernels: 0 us -> 196 us
  other arithmetic: 139 us -> 18.5 us
  blocking collectives: 38 us -> 0 us
  local copies, waits for them, and re-layouts: 53.3 us -> 19 us
  starting transfers between devices: 31.8 us -> 10 us
  waiting for transfers between devices: 11.5 us -> 24 us
    pallas_call x0 -> x2, Pallas kernels: none -> 196 us  [the longest x1 186 us: local(): pl.pallas_call(functools.partial(window_kernel, hours, width, rim), out_s...]
    div x25 -> x0, other arithmetic: 47.7 us -> none  [the longest x24 46.5 us: face_flux(): -jnp.power(mean_depth, 5.0 / 3.0) * slope]
    psum x2 -> x0, blocking collectives: 38 us -> none  [the longest x1 32.3 us: local(): summed = lax.psum((misfit, cells), 'space')]
    add x25 -> x0, other arithmetic: 33.1 us -> none  [the longest x12 22.2 us: advance_big(): level = padded + ground_big[None]]
    while x72 -> x0, local copies, waits for them, and re-layouts: 28.6 us -> none
    mul x25 -> x2, other arithmetic: 15.3 us -> 0.01 us  [the longest x1 0.01 us: local(): time_step * conduct * suction_p]
    all_gather x1, waiting for transfers between devices: 0.37 us -> 15.5 us  [local(): lax.all_gather(forcing, 'dom', axis=3, tiled=True)[:, :, 0]]
    ppermute x12 -> x4, starting transfers between devices: 21.5 us -> 7.38 us  [passed_along_2(): lax.ppermute(array, axis, [(i, (i + by) % devices) for i in range(devices)])]
  transfers between devices with their start and end apart: 19 -> 7, of which waited for: 5 -> 3; matrix products, arithmetic and copies ran while one was open for 10% -> 6% of each run, Pallas kernels for 0% -> 0%
where the time goes in v1:
time: 284 us; the launch traced here: 283 us
  Pallas kernels  196 us (69%)
  waiting for transfers between devices  24 us (8%)
  local copies, waits for them, and re-layouts  19 us (7%)
  other arithmetic  18.5 us (7%)
  between operations  15.6 us (5%)
  starting transfers between devices  10 us (4%)
    pallas_call x1, Pallas kernels, local(): pl.pallas_call(functools.partial(window_kernel, hours, width, rim), out_s...  186 us
    all_gather x1, waiting for transfers between devices, local(): lax.all_gather(forcing, 'dom', axis=3, tiled=True)[:, :, 0]  15.5 us
    pallas_call x1, Pallas kernels, local(): pl.pallas_call(functools.partial(weigh_kernel, n_space, n_dom, parts), ou...  10.2 us
    ppermute x2, waiting for transfers between devices, passed_along(): return lax.ppermute(block, axis, route)  8.48 us
    ppermute x4, starting transfers between devices, passed_along_2(): lax.ppermute(array, axis, [(i, (i + by) % devices) for i in range(devices)])  7.38 us
    ppermute x4, local copies, waits for them, and re-layouts, passed_along_2(): lax.ppermute(array, axis, [(i, (i + by) % devices) for i in range(devices)])  6.87 us
  transfers between devices with their start and end apart: 7, of which 3 were waited for; matrix products, arithmetic and copies ran while one was open for 6% of the time, Pallas kernels for 0%

profile of v1, /device:TPU:0, one launch (start us, length us, event | category | flops | bytes accessed | tf_op | source)
XLA Modules:
  0.0 283.2 jit_solution(5337525172038695778)
XLA Ops:
  7.2 0.0 copy-start
  7.2 0.0 copy-start.10
  7.2 0.0 copy-start.11
  7.2 0.0 copy-start.12
  7.2 0.0 copy-start.7
  7.2 0.0 all-gather.2.cloned.1.call-start
  7.3 2.0 copy.36
  9.2 0.0 all-gather.2.cloned.1.call-update
  9.3 0.7 compare_and_fusion
  9.9 1.3 gather_fusion
  11.2 0.0 copy-done
  11.2 0.6 gather_fusion.1
  11.9 2.8 gather_fusion.2
  14.7 0.0 copy-done.10
  14.7 0.0 copy-done.12
  14.7 0.7 select_reduce_fusion.2
  15.4 0.0 copy-done.7
  15.4 0.7 convert_reduce_fusion
  16.1 2.5 broadcast_select_fusion.1
  18.7 15.5 %all-gather.2.cloned.1.call-done = bf16[2,2,1,256,512]{4,3,0,1,2:T(8,128)(2,1)} async-done(((bf16[2,2,1,128,512]{4,3,0,1,2:T(8,128)(2,1)}), bf16[2,2,1,256,512]{4,3,0,1,2:T(8,128)(2,1)}) %all-gather.2.cloned.1.call-update) | async-done | bytes 1048592 | tf_op jit(solution)/shard_map/all_gather | solution.py:239
  34.2 1.6 bitcast_convert_fusion
  35.8 0.0 copy-start.14
  35.8 1.4 convert_select_fusion
  37.2 0.0 copy-start.3
  37.2 2.9 %pad_maximum_fusion.4 = (f32[7,256,12]{2,1,0:T(8,128)}, f32[7,256,12]{2,1,0:T(8,128)}) fusion(f32[2,256,512]{2,1,0:T(8,128)S(1)} %get-tuple-element.73, f32[1,256,512]{2,1,0:T(8,128)} %param.23, f32[2,256,512]{2,1,0:T(8,128)S(1)} %copy-done.1, f32[2,256,512]{2,1,0:T(8,128)S(1)} %get-tuple-element.76), kind=kLoop, calls=%fused_computation.13 | loop fusion | flops 129024 | bytes 3842048 | tf_op jit(solution)/shard_map/slice | solution.py:244
  40.1 1.5 copy.41
  41.6 2.8 collective-permute-start.2
  44.4 1.6 collective-permute-start.3
  46.7 0.6 reduce_sum.62
  47.9 0.0 copy-start.9
  47.9 1.5 copy.37
  49.4 0.1 collective-permute-start
  49.5 2.9 %collective-permute-start.1 = (f32[7,256,12]{1,0,2:T(8,128)S(1)}, f32[7,256,12]{1,0,2:T(8,128)}, u32[]{:S(2)}, u32[]{:S(2)}) collective-permute-start(f32[7,256,12]{1,0,2:T(8,128)S(1)} %copy.37), channel_id=1, source_target_pairs={{0,30},{2,0},{4,2},{6,4},{8,6},{10,8},{12,10},{14,12},{16,14},{18,... | collective-permute-start | bytes 258056 | tf_op jit(solution)/shard_map/ppermute | solution.py:31
  52.4 0.0 collective-permute-done.2
  52.4 1.3 copy.43
  53.7 0.0 collective-permute-done.3
  53.7 1.3 copy.44
  54.9 2.2 broadcast_select_fusion.2
  57.2 0.0 collective-permute-done
  57.2 2.1 copy.39
  59.3 0.0 collective-permute-done.1
  59.3 2.2 copy.40
  61.5 1.3 broadcast_select_fusion.3
  62.8 0.0 copy-start.2
  62.8 0.0 copy-start.4
  62.8 0.0 copy-start.6
  62.9 0.1 broadcast_in_dim.99
  63.0 1.3 pad_maximum_fusion.11
  64.3 1.3 collective-permute-start.4
  65.6 1.3 collective-permute-start.5
  67.0 4.4 %collective-permute-done.4 = f32[7,16,640]{2,1,0:T(8,128)S(1)} collective-permute-done((f32[7,16,640]{2,1,0:T(8,128)S(1)}, f32[7,16,640]{2,1,0:T(8,128)S(1)}, u32[]{:S(2)}, u32[]{:S(2)}) %collective-permute-start.4) | collective-permute-done | bytes 286752 | tf_op jit(solution)/shard_map/ppermute | solution.py:26
  71.3 4.1 %collective-permute-done.5 = f32[7,16,640]{2,1,0:T(8,128)S(1)} collective-permute-done((f32[7,16,640]{2,1,0:T(8,128)S(1)}, f32[7,16,640]{2,1,0:T(8,128)S(1)}, u32[]{:S(2)}, u32[]{:S(2)}) %collective-permute-start.5) | collective-permute-done | bytes 286752 | tf_op jit(solution)/shard_map/ppermute | solution.py:26
  75.4 0.1 broadcast_select_fusion.5
  75.6 0.0 copy-done.2
  75.6 0.0 copy-done.4
  75.6 0.0 copy-done.5
  75.6 0.0 copy-done.6
  75.6 2.3 pad_maximum_fusion
  78.0 0.3 fusion.3
  78.3 185.8 %shard_map.148 = (f32[2,256,512]{2,1,0:T(8,128)}, f32[2,256,512]{2,1,0:T(8,128)}, f32[2,8,128]{2,1,0:T(8,128)S(1)}) custom-call(f32[3,2]{1,0:T(4,128)S(1)} %pad_maximum_fusion.12.par_ref, f32[2,288,640]{2,1,0:T(8,128)S(1)} %get-tuple-element.69.d_in, f32[2,288,640]{2,1,0:T(8,128)S(1)} %get-tuple-element.68.s_in, f32[288,640]{1,0:T(8,128)S(1)} %slice_bitcast_fusion.g_ref, ...), custom_call_target="tpu_custom_call" | custom-call | tf_op jit(solution)/shard_map/pallas_call | solution.py:255
  264.1 0.1 reduce_sum.60
  264.3 0.6 copy-done.8
  264.9 10.2 %shard_map.149 = f32[8,128]{1,0:T(8,128)} custom-call(f32[8,128]{1,0:T(8,128)} %copy-done.8), custom_call_target="tpu_custom_call" | custom-call | tf_op jit(solution)/shard_map/pallas_call | solution.py:276
  275.1 1.2 slice_bitcast_fusion.1
  (21 shorter events, 0.2 us)
Async XLA Ops:
  7.2 4.1 %copy-start = (f32[2,1,256,512]{3,2,1,0:T(8,128)S(1)}, f32[2,1,256,512]{3,2,1,0:T(8,128)}, u32[]{:S(2)}) copy-start(f32[2,1,256,512]{3,2,1,0:T(8,128)} %param.21) | copy-start | bytes 3145732
  7.2 7.5 %copy-start.10 = (f32[4]{0:T(128)S(1)}, f32[4]{0:T(128)}, u32[]{:S(2)}) copy-start(f32[4]{0:T(128)} %param.29) | copy-start | bytes 52
  7.2 7.5 %copy-start.11 = (f32[4]{0:T(128)S(1)}, f32[4]{0:T(128)}, u32[]{:S(2)}) copy-start(f32[4]{0:T(128)} %param.28) | copy-start | bytes 52
  7.2 7.5 %copy-start.12 = (f32[4]{0:T(128)S(1)}, f32[4]{0:T(128)}, u32[]{:S(2)}) copy-start(f32[4]{0:T(128)} %param.27) | copy-start | bytes 52
  7.2 8.2 %copy-start.7 = (s32[1,256,512]{2,1,0:T(8,128)S(1)}, s32[1,256,512]{2,1,0:T(8,128)}, u32[]{:S(2)}) copy-start(s32[1,256,512]{2,1,0:T(8,128)} %param.24) | copy-start | bytes 1572868
  7.2 27.0 %all-gather.2.cloned.1.call-start = ((), (), s32[]{:S(2)}) async-start(), calls=%async_computation | async-start | bytes 1572864 | tf_op jit(solution)/shard_map/all_gather | solution.py:239
  34.2 3.0 %copy-start.1 = (f32[2,256,512]{2,1,0:T(8,128)S(1)}, f32[2,256,512]{2,1,0:T(8,128)}, u32[]{:S(2)}) copy-start(f32[2,256,512]{2,1,0:T(8,128)} %get-tuple-element.77) | copy-start | bytes 3145732
  35.8 10.9 %copy-start.14 = (f32[2]{0:T(128)S(1)}, f32[2]{0:T(128)}, u32[]{:S(2)}) copy-start(f32[2]{0:T(128)} %param.32) | copy-start | bytes 28
  37.2 2.9 %copy-start.3 = (f32[2,256,512]{2,1,0:T(8,128)}, f32[2,256,512]{2,1,0:T(8,128)S(1)}, u32[]{:S(2)}) copy-start(f32[2,256,512]{2,1,0:T(8,128)S(1)} %get-tuple-element.73) | copy-start | bytes 3145732
  41.6 10.8 %collective-permute-start.2 = (f32[7,256,12]{1,0,2:T(8,128)S(1)}, f32[7,256,12]{1,0,2:T(8,128)S(1)}, u32[]{:S(2)}, u32[]{:S(2)}) collective-permute-start(f32[7,256,12]{1,0,2:T(8,128)S(1)} %copy.41), channel_id=1, source_target_pairs={{0,26},{2,28},{4,30},{6,0},{8,2},{10,4},{12,6},{14,8},{16,10},{18,... | collective-permute-start | bytes 258056 | tf_op jit(solution)/shard_map/ppermute | solution.py:31
  44.4 9.2 %collective-permute-start.3 = (f32[7,256,12]{1,0,2:T(8,128)S(1)}, f32[7,256,12]{1,0,2:T(8,128)S(1)}, u32[]{:S(2)}, u32[]{:S(2)}) collective-permute-start(f32[7,256,12]{1,0,2:T(8,128)S(1)} %copy.41), channel_id=1, source_target_pairs={{0,2},{2,4},{4,6},{6,8},{8,10},{10,12},{12,14},{14,16},{16,18},{18... | collective-permute-start | bytes 258056 | tf_op jit(solution)/shard_map/ppermute | solution.py:31
  47.9 14.9 %copy-start.9 = (f32[7]{0:T(128)S(1)}, f32[7]{0:T(128)}, u32[]{:S(2)}) copy-start(f32[7]{0:T(128)} %constant.158.clone) | copy-start | bytes 88
  49.4 7.7 %collective-permute-start = (f32[7,256,12]{1,0,2:T(8,128)S(1)}, f32[7,256,12]{1,0,2:T(8,128)}, u32[]{:S(2)}, u32[]{:S(2)}) collective-permute-start(f32[7,256,12]{1,0,2:T(8,128)S(1)} %copy.37), channel_id=1, source_target_pairs={{0,6},{2,8},{4,10},{6,12},{8,14},{10,16},{12,18},{14,20},{16,22},{... | collective-permute-start | bytes 258056 | tf_op jit(solution)/shard_map/ppermute | solution.py:31
  49.5 9.8 %collective-permute-start.1 = (f32[7,256,12]{1,0,2:T(8,128)S(1)}, f32[7,256,12]{1,0,2:T(8,128)}, u32[]{:S(2)}, u32[]{:S(2)}) collective-permute-start(f32[7,256,12]{1,0,2:T(8,128)S(1)} %copy.37), channel_id=1, source_target_pairs={{0,30},{2,0},{4,2},{6,4},{8,6},{10,8},{12,10},{14,12},{16,14},{18,... | collective-permute-start | bytes 258056 | tf_op jit(solution)/shard_map/ppermute | solution.py:31
  61.5 5.4 %copy-start.13 = (f32[2]{0:T(128)S(1)}, f32[2]{0:T(128)}, u32[]{:S(2)}) copy-start(f32[2]{0:T(128)} %get-tuple-element.59) | copy-start | bytes 28
  62.8 12.8 %copy-start.2 = (f32[2,256,512]{2,1,0:T(8,128)S(1)}, f32[2,256,512]{2,1,0:T(8,128)}, u32[]{:S(2)}) copy-start(f32[2,256,512]{2,1,0:T(8,128)} %get-tuple-element.77) | copy-start | bytes 3145732
  62.8 12.7 %copy-start.4 = (f32[2,256,512]{2,1,0:T(8,128)S(1)}, f32[2,256,512]{2,1,0:T(8,128)}, u32[]{:S(2)}) copy-start(f32[2,256,512]{2,1,0:T(8,128)} %copy-done.3) | copy-start | bytes 3145732
  62.8 12.7 %copy-start.5 = (f32[7,256,12]{2,1,0:T(8,128)S(1)}, f32[7,256,12]{2,1,0:T(8,128)}, u32[]{:S(2)}) copy-start(f32[7,256,12]{2,1,0:T(8,128)} %broadcast_select_fusion.2) | copy-start | bytes 258052
  62.8 12.7 %copy-start.6 = (f32[1,256,512]{2,1,0:T(8,128)S(1)}, f32[1,256,512]{2,1,0:T(8,128)}, u32[]{:S(2)}) copy-start(f32[1,256,512]{2,1,0:T(8,128)} %param.23) | copy-start | bytes 1572868
  64.3 7.0 %collective-permute-start.4 = (f32[7,16,640]{2,1,0:T(8,128)S(1)}, f32[7,16,640]{2,1,0:T(8,128)S(1)}, u32[]{:S(2)}, u32[]{:S(2)}) collective-permute-start(f32[7,16,640]{2,1,0:T(8,128)S(1)} %get-tuple-element.65), channel_id=1, source_target_pairs={{0,8},{2,10},{4,12},{6,14},{8,16},{10,18},{12,20},{14,22},{16,24},... | collective-permute-start | bytes 860168 | tf_op jit(solution)/shard_map/ppermute | solution.py:26
  65.6 9.8 %collective-permute-start.5 = (f32[7,16,640]{2,1,0:T(8,128)S(1)}, f32[7,16,640]{2,1,0:T(8,128)S(1)}, u32[]{:S(2)}, u32[]{:S(2)}) collective-permute-start(f32[7,16,640]{2,1,0:T(8,128)S(1)} %get-tuple-element.66), channel_id=1, source_target_pairs={{8,0},{10,2},{12,4},{14,6},{16,8},{18,10},{20,12},{22,14},{24,16},... | collective-permute-start | bytes 860168 | tf_op jit(solution)/shard_map/ppermute | solution.py:26
  264.3 0.6 copy-start.8
Sparse Core Ops, SparseCore 0:
  10.2 23.9 all-gather.1

commit v2 on v1

--- a/solution.py
+++ b/solution.py
@@ -50,7 +50,7 @@
 
 def window_kernel(
     hours, width, rim, par_ref, d_in, s_in, g_ref, r_ref, obs_ref,
-    depth_out, soak_out, miss_out, d_ref, s_ref, ge_ref, gs_ref,
+    depth_out, soak_out, miss_out, d_ref, s_ref, d_two, s_two, ge_ref, gs_ref,
 ):
     parts, high, wide = d_in.shape
     own_rows, own_cols = depth_out.shape[1:]
@@ -86,49 +86,54 @@
     lax.fori_loop(0, blocks, prepare, 0)
     for p in range(parts):
         d_ref[p, pl.ds(high, ROWS), :] = jnp.zeros((ROWS, wide), jnp.float32)
+        d_two[p, pl.ds(high, ROWS), :] = jnp.zeros((ROWS, wide), jnp.float32)
+    several = next(u for u in (4, 3, 2, 1) if blocks % u == 0)
 
     for hour in range(hours):
 
-        def substep(index, carry):
-            left = hours * SUB - 1 - (hour * SUB + index)
-            start = top - 1 - left // ROWS
-            stop = bottom + (left + ROWS - 1) // ROWS
-
+        def substep(d_old, s_old, d_new, s_new):
             def step(block, above):
                 out = []
                 for p in range(parts):
                     k, a, b = par_ref[0, p], par_ref[1, p], par_ref[2, p]
-                    d = [d_ref[(p,) + at(block, j)] for j in range(cols)]
+                    d = [d_old[(p,) + at(block, j)] for j in range(cols)]
 
                     def col_face(j):
                         d_e = east(d[j], d[(j + 1) % cols])
                         return face(d[j] + d_e, (d_e - d[j]) + ge_ref[at(block, j)])
 
-                    last = col_face(cols - 1)
-                    west = last
+                    f_col = [col_face(j) for j in range(cols)]
                     for j in range(cols):
-                        f_e = last if j == cols - 1 else col_face(j)
-                        f_w = pltpu.roll(jnp.where(last_lane, west, f_e), 1, 1)
-                        west = f_e
-                        d_s = south(d[j], d_ref[(p,) + at(block + 1, j)])
+                        f_e = f_col[j]
+                        f_w = pltpu.roll(jnp.where(last_lane, f_col[j - 1], f_e), 1, 1)
+                        d_s = south(d[j], d_old[(p,) + at(block + 1, j)])
                         f_s = face(d[j] + d_s, (d_s - d[j]) + gs_ref[at(block, j)])
                         f_n = pltpu.roll(jnp.where(last_sub, above[p * cols + j], f_s), 1, 0)
                         out.append(f_s)
                         gain = (f_e - f_w) + (f_s - f_n)
                         ponded = jnp.maximum(d[j] + k * gain + r_ref[(hour,) + at(block, j)], 0.0)
-                        soak = s_ref[(p,) + at(block, j)]
+                        soak = s_old[(p,) + at(block, j)]
                         inverse = pl.reciprocal(soak, approx=True)
                         inverse = inverse * (2.0 - soak * inverse)
                         intake = jnp.minimum(a + b * inverse, ponded)
-                        d_ref[(p,) + at(block, j)] = ponded - intake
-                        s_ref[(p,) + at(block, j)] = soak + intake
+                        d_new[(p,) + at(block, j)] = ponded - intake
+                        s_new[(p,) + at(block, j)] = soak + intake
                 return tuple(out)
 
+            def steps(index, above):
+                for u in range(several):
+                    above = step(index * several + u, above)
+                return above
+
             zero = jnp.zeros((ROWS, LANES), jnp.float32)
-            lax.fori_loop(start, stop, step, (zero,) * (parts * cols))
+            lax.fori_loop(0, blocks // several, steps, (zero,) * (parts * cols))
+
+        def pair(index, carry):
+            substep(d_ref, s_ref, d_two, s_two)
+            substep(d_two, s_two, d_ref, s_ref)
             return carry
 
-        lax.fori_loop(0, SUB, substep, 0)
+        lax.fori_loop(0, SUB // 2, pair, 0)
 
         def score(block, sums):
             sums = list(sums)
@@ -264,6 +269,8 @@
         scratch_shapes=[
             pltpu.VMEM((parts, high + ROWS, across), jnp.float32),
             pltpu.VMEM((parts, high, across), jnp.float32),
+            pltpu.VMEM((parts, high + ROWS, across), jnp.float32),
+            pltpu.VMEM((parts, high, across), jnp.float32),
             pltpu.VMEM((high, across), jnp.float32),
             pltpu.VMEM((high, across), jnp.float32),
         ],

time: 284 us -> 140 us (0.49)
  Pallas kernels: 196 us -> 52.3 us
    pallas_call x1, Pallas kernels: 186 us -> 42.1 us  [local(): pl.pallas_call(functools.partial(window_kernel, hours, width, rim), out_s...]
  transfers between devices with their start and end apart: 7 -> 7, of which waited for: 3 -> 3; matrix products, arithmetic and copies ran while one was open for 6% -> 13% of each run, Pallas kernels for 0% -> 0%
where the time goes in v2:
time: 140 us; the launch traced here: 139 us
  Pallas kernels  52.3 us (37%)
  waiting for transfers between devices  24 us (17%)
  local copies, waits for them, and re-layouts  19 us (14%)
  other arithmetic  18.5 us (13%)
  between operations  15.6 us (11%)
  starting transfers between devices  10 us (7%)
    pallas_call x1, Pallas kernels, local(): pl.pallas_call(functools.partial(window_kernel, hours, width, rim), out_s...  42.1 us
    all_gather x1, waiting for transfers between devices, local(): lax.all_gather(forcing, 'dom', axis=3, tiled=True)[:, :, 0]  15.5 us
    pallas_call x1, Pallas kernels, local(): pl.pallas_call(functools.partial(weigh_kernel, n_space, n_dom, parts), ou...  10.2 us
    ppermute x2, waiting for transfers between devices, passed_along(): return lax.ppermute(block, axis, route)  8.48 us
    ppermute x4, starting transfers between devices, passed_along_2(): lax.ppermute(array, axis, [(i, (i + by) % devices) for i in range(devices)])  7.38 us
    ppermute x4, local copies, waits for them, and re-layouts, passed_along_2(): lax.ppermute(array, axis, [(i, (i + by) % devices) for i in range(devices)])  6.87 us
    slice x1, other arithmetic, local(): east = from_east(fields[:, :, :width], column_tile)  2.88 us
    gather x1, local copies, waits for them, and re-layouts, local(): soaked = jnp.take(infiltrated[:, 0], local_slot, axis=0)  2.81 us
  transfers between devices with their start and end apart: 7, of which 3 were waited for; matrix products, arithmetic and copies ran while one was open for 13% of the time, Pallas kernels for 0%

profile of v2, /device:TPU:0, one launch (start us, length us, event | category | flops | bytes accessed | tf_op | source)
XLA Modules:
  0.0 139.4 jit_solution(6026145196386401428)
XLA Ops:
  7.2 0.0 copy-start
  7.2 0.0 copy-start.10
  7.2 0.0 copy-start.11
  7.2 0.0 copy-start.12
  7.2 0.0 copy-start.7
  7.2 0.0 all-gather.2.cloned.1.call-start
  7.3 2.0 %copy.36 = bf16[2,2,1,128,512]{4,3,0,1,2:T(8,128)(2,1)} copy(bf16[2,2,1,128,512]{4,3,2,1,0:T(8,128)(2,1)} %param.25) | data formatting | bytes 1048576 | tf_op args[4]
  9.2 0.0 all-gather.2.cloned.1.call-update
  9.3 0.7 compare_and_fusion
  9.9 1.3 gather_fusion
  11.2 0.0 copy-done
  11.2 0.6 gather_fusion.1
  11.9 2.8 %gather_fusion.2 = f32[2,256,512]{2,1,0:T(8,128)} fusion(f32[2,256,512]{2,1,0:T(8,128)} %bitcast.35, s32[1024]{0:T(1024)S(1)} %pad_clamp_fusion), kind=kCustom, calls=%fused_computation.1.clone | custom fusion | bytes 2097160 | tf_op jit(solution)/shard_map/jit(_take)/gather | solution.py:228
  14.7 0.0 copy-done.10
  14.7 0.0 copy-done.12
  14.7 0.7 select_reduce_fusion.2
  15.4 0.0 copy-done.7
  15.4 0.7 convert_reduce_fusion
  16.1 2.5 %broadcast_select_fusion.1 = (f32[2,256,512]{2,1,0:T(8,128)S(1)}, f32[2,256,512]{2,1,0:T(8,128)}) fusion(f32[2,256,512]{2,1,0:T(8,128)S(1)} %gather_fusion.1, pred[2]{0:T(512)(128)(4,1)S(1)} %get-tuple-element.63, f32[2,256,512]{2,1,0:T(8,128)} %gather_fusion.2), kind=kLoop, calls=%fused_computation.16 | loop fusion | flops 524288 | bytes 4194306 | tf_op jit(solution)/shard_map/jit(_take)/select_n | solution.py:227
  18.7 15.5 %all-gather.2.cloned.1.call-done = bf16[2,2,1,256,512]{4,3,0,1,2:T(8,128)(2,1)} async-done(((bf16[2,2,1,128,512]{4,3,0,1,2:T(8,128)(2,1)}), bf16[2,2,1,256,512]{4,3,0,1,2:T(8,128)(2,1)}) %all-gather.2.cloned.1.call-update) | async-done | bytes 1048592 | tf_op jit(solution)/shard_map/all_gather | solution.py:244
  34.2 1.6 %bitcast_convert_fusion = f32[2,2,256,512]{3,2,0,1:T(8,128)S(1)} fusion(bf16[2,2,1,256,512]{4,3,0,1,2:T(8,128)(2,1)} %all-gather.2.cloned.1.call-done), kind=kLoop, calls=%fused_computation.9 | loop fusion | flops 524288 | bytes 3145728 | tf_op jit(solution)/shard_map/convert_element_type | solution.py:244
  35.8 0.0 copy-start.14
  35.8 1.4 convert_select_fusion
  37.2 0.0 copy-start.3
  37.2 2.9 %pad_maximum_fusion.4 = (f32[7,256,12]{2,1,0:T(8,128)}, f32[7,256,12]{2,1,0:T(8,128)}) fusion(f32[2,256,512]{2,1,0:T(8,128)S(1)} %get-tuple-element.73, f32[1,256,512]{2,1,0:T(8,128)} %param.23, f32[2,256,512]{2,1,0:T(8,128)S(1)} %copy-done.1, f32[2,256,512]{2,1,0:T(8,128)S(1)} %get-tuple-element.76), kind=kLoop, calls=%fused_computation.13 | loop fusion | flops 129024 | bytes 3842048 | tf_op jit(solution)/shard_map/slice | solution.py:249
  40.1 1.5 %copy.41 = f32[7,256,12]{1,0,2:T(8,128)S(1)} copy(f32[7,256,12]{2,1,0:T(8,128)} %get-tuple-element.71) | data formatting | bytes 172032 | tf_op jit(solution)/shard_map/slice | solution.py:248
  41.6 2.8 %collective-permute-start.2 = (f32[7,256,12]{1,0,2:T(8,128)S(1)}, f32[7,256,12]{1,0,2:T(8,128)S(1)}, u32[]{:S(2)}, u32[]{:S(2)}) collective-permute-start(f32[7,256,12]{1,0,2:T(8,128)S(1)} %copy.41), channel_id=1, source_target_pairs={{0,26},{2,28},{4,30},{6,0},{8,2},{10,4},{12,6},{14,8},{16,10},{18,... | collective-permute-start | bytes 258056 | tf_op jit(solution)/shard_map/ppermute | solution.py:31
  44.4 1.6 %collective-permute-start.3 = (f32[7,256,12]{1,0,2:T(8,128)S(1)}, f32[7,256,12]{1,0,2:T(8,128)S(1)}, u32[]{:S(2)}, u32[]{:S(2)}) collective-permute-start(f32[7,256,12]{1,0,2:T(8,128)S(1)} %copy.41), channel_id=1, source_target_pairs={{0,2},{2,4},{4,6},{6,8},{8,10},{10,12},{12,14},{14,16},{16,18},{18... | collective-permute-start | bytes 258056 | tf_op jit(solution)/shard_map/ppermute | solution.py:31
  46.7 0.6 reduce_sum.62
  47.9 0.0 copy-start.9
  47.9 1.5 %copy.37 = f32[7,256,12]{1,0,2:T(8,128)S(1)} copy(f32[7,256,12]{2,1,0:T(8,128)} %get-tuple-element.70) | data formatting | bytes 172032 | tf_op jit(solution)/shard_map/slice | solution.py:249
  49.4 0.1 collective-permute-start
  49.5 2.9 %collective-permute-start.1 = (f32[7,256,12]{1,0,2:T(8,128)S(1)}, f32[7,256,12]{1,0,2:T(8,128)}, u32[]{:S(2)}, u32[]{:S(2)}) collective-permute-start(f32[7,256,12]{1,0,2:T(8,128)S(1)} %copy.37), channel_id=1, source_target_pairs={{0,30},{2,0},{4,2},{6,4},{8,6},{10,8},{12,10},{14,12},{16,14},{18,... | collective-permute-start | bytes 258056 | tf_op jit(solution)/shard_map/ppermute | solution.py:31
  52.4 0.0 collective-permute-done.2
  52.4 1.3 copy.43
  53.7 0.0 collective-permute-done.3
  53.7 1.3 copy.44
  54.9 2.2 %broadcast_select_fusion.2 = f32[7,256,12]{2,1,0:T(8,128)} fusion(f32[7,256,12]{2,1,0:T(8,128)} %copy.43, f32[7,256,12]{2,1,0:T(8,128)} %copy.44, pred[]{:T(512)S(6)} %eq.32), kind=kLoop, calls=%fused_computation.18 | loop fusion | flops 21504 | bytes 258049 | tf_op jit(solution)/shard_map/jit(_where)/select_n | solution.py:37
  57.2 0.0 collective-permute-done
  57.2 2.1 %copy.39 = f32[7,256,12]{2,1,0:T(8,128)} copy(f32[7,256,12]{1,0,2:T(8,128)} %collective-permute-done) | data formatting | bytes 172032 | tf_op jit(solution)/shard_map/ppermute | solution.py:31
  59.3 0.0 collective-permute-done.1
  59.3 2.2 %copy.40 = f32[7,256,12]{2,1,0:T(8,128)} copy(f32[7,256,12]{1,0,2:T(8,128)} %collective-permute-done.1) | data formatting | bytes 172032 | tf_op jit(solution)/shard_map/ppermute | solution.py:31
  61.5 1.3 broadcast_select_fusion.3
  62.8 0.0 copy-start.2
  62.8 0.0 copy-start.4
  62.8 0.0 copy-start.6
  62.9 0.1 broadcast_in_dim.99
  63.0 1.3 pad_maximum_fusion.11
  64.3 1.3 collective-permute-start.4
  65.6 1.3 collective-permute-start.5
  67.0 4.4 %collective-permute-done.4 = f32[7,16,640]{2,1,0:T(8,128)S(1)} collective-permute-done((f32[7,16,640]{2,1,0:T(8,128)S(1)}, f32[7,16,640]{2,1,0:T(8,128)S(1)}, u32[]{:S(2)}, u32[]{:S(2)}) %collective-permute-start.4) | collective-permute-done | bytes 286752 | tf_op jit(solution)/shard_map/ppermute | solution.py:26
  71.3 4.1 %collective-permute-done.5 = f32[7,16,640]{2,1,0:T(8,128)S(1)} collective-permute-done((f32[7,16,640]{2,1,0:T(8,128)S(1)}, f32[7,16,640]{2,1,0:T(8,128)S(1)}, u32[]{:S(2)}, u32[]{:S(2)}) %collective-permute-start.5) | collective-permute-done | bytes 286752 | tf_op jit(solution)/shard_map/ppermute | solution.py:26
  75.4 0.1 broadcast_select_fusion.5
  75.6 0.0 copy-done.2
  75.6 0.0 copy-done.4
  75.6 0.0 copy-done.5
  75.6 0.0 copy-done.6
  75.6 2.3 %pad_maximum_fusion = f32[7,288,640]{2,1,0:T(8,128)S(1)} fusion(f32[7,16,640]{2,1,0:T(8,128)S(1)} %get-tuple-element.75, f32[7,256,12]{2,1,0:T(8,128)S(1)} %copy-done.5, f32[7,256,104]{2,1,0:T(8,128)S(1)} %broadcast_in_dim.99, f32[7,256,12]{2,1,0:T(8,128)S(1)} %broadcast_select_fusion.3, f32[2,256,512]{2,1,0:T(8,128)S(1)} %copy-done.4, ...), kind=kLoop, calls=%fused_computation.3 | loop fusion | flops 10321920 | bytes 10321920 | tf_op jit(solution)/shard_map/concatenate | solution.py:256
  78.0 0.3 fusion.3
  78.3 42.1 %shard_map.148 = (f32[2,256,512]{2,1,0:T(8,128)}, f32[2,256,512]{2,1,0:T(8,128)}, f32[2,8,128]{2,1,0:T(8,128)S(1)}) custom-call(f32[3,2]{1,0:T(4,128)S(1)} %pad_maximum_fusion.12.par_ref, f32[2,288,640]{2,1,0:T(8,128)S(1)} %get-tuple-element.69.d_in, f32[2,288,640]{2,1,0:T(8,128)S(1)} %get-tuple-element.68.s_in, f32[288,640]{1,0:T(8,128)S(1)} %slice_bitcast_fusion.g_ref, ...), custom_call_target="tpu_custom_call" | custom-call | tf_op jit(solution)/shard_map/pallas_call | solution.py:260
  120.4 0.1 reduce_sum.60
  120.6 0.6 copy-done.8
  121.2 10.2 %shard_map.149 = f32[8,128]{1,0:T(8,128)} custom-call(f32[8,128]{1,0:T(8,128)} %copy-done.8), custom_call_target="tpu_custom_call" | custom-call | tf_op jit(solution)/shard_map/pallas_call | solution.py:283
  131.4 1.2 slice_bitcast_fusion.1
  (21 shorter events, 0.2 us)
Async XLA Ops:
  7.2 4.1 %copy-start = (f32[2,1,256,512]{3,2,1,0:T(8,128)S(1)}, f32[2,1,256,512]{3,2,1,0:T(8,128)}, u32[]{:S(2)}) copy-start(f32[2,1,256,512]{3,2,1,0:T(8,128)} %param.21) | copy-start | bytes 3145732
  7.2 7.5 %copy-start.10 = (f32[4]{0:T(128)S(1)}, f32[4]{0:T(128)}, u32[]{:S(2)}) copy-start(f32[4]{0:T(128)} %param.29) | copy-start | bytes 52
  7.2 7.5 %copy-start.11 = (f32[4]{0:T(128)S(1)}, f32[4]{0:T(128)}, u32[]{:S(2)}) copy-start(f32[4]{0:T(128)} %param.28) | copy-start | bytes 52
  7.2 7.5 %copy-start.12 = (f32[4]{0:T(128)S(1)}, f32[4]{0:T(128)}, u32[]{:S(2)}) copy-start(f32[4]{0:T(128)} %param.27) | copy-start | bytes 52
  7.2 8.2 %copy-start.7 = (s32[1,256,512]{2,1,0:T(8,128)S(1)}, s32[1,256,512]{2,1,0:T(8,128)}, u32[]{:S(2)}) copy-start(s32[1,256,512]{2,1,0:T(8,128)} %param.24) | copy-start | bytes 1572868
  7.2 27.0 %all-gather.2.cloned.1.call-start = ((), (), s32[]{:S(2)}) async-start(), calls=%async_computation | async-start | bytes 1572864 | tf_op jit(solution)/shard_map/all_gather | solution.py:244
  34.2 3.0 %copy-start.1 = (f32[2,256,512]{2,1,0:T(8,128)S(1)}, f32[2,256,512]{2,1,0:T(8,128)}, u32[]{:S(2)}) copy-start(f32[2,256,512]{2,1,0:T(8,128)} %get-tuple-element.77) | copy-start | bytes 3145732
  35.8 10.9 %copy-start.14 = (f32[2]{0:T(128)S(1)}, f32[2]{0:T(128)}, u32[]{:S(2)}) copy-start(f32[2]{0:T(128)} %param.32) | copy-start | bytes 28
  37.2 2.9 %copy-start.3 = (f32[2,256,512]{2,1,0:T(8,128)}, f32[2,256,512]{2,1,0:T(8,128)S(1)}, u32[]{:S(2)}) copy-start(f32[2,256,512]{2,1,0:T(8,128)S(1)} %get-tuple-element.73) | copy-start | bytes 3145732
  41.6 10.8 %collective-permute-start.2 = (f32[7,256,12]{1,0,2:T(8,128)S(1)}, f32[7,256,12]{1,0,2:T(8,128)S(1)}, u32[]{:S(2)}, u32[]{:S(2)}) collective-permute-start(f32[7,256,12]{1,0,2:T(8,128)S(1)} %copy.41), channel_id=1, source_target_pairs={{0,26},{2,28},{4,30},{6,0},{8,2},{10,4},{12,6},{14,8},{16,10},{18,... | collective-permute-start | bytes 258056 | tf_op jit(solution)/shard_map/ppermute | solution.py:31
  44.4 9.2 %collective-permute-start.3 = (f32[7,256,12]{1,0,2:T(8,128)S(1)}, f32[7,256,12]{1,0,2:T(8,128)S(1)}, u32[]{:S(2)}, u32[]{:S(2)}) collective-permute-start(f32[7,256,12]{1,0,2:T(8,128)S(1)} %copy.41), channel_id=1, source_target_pairs={{0,2},{2,4},{4,6},{6,8},{8,10},{10,12},{12,14},{14,16},{16,18},{18... | collective-permute-start | bytes 258056 | tf_op jit(solution)/shard_map/ppermute | solution.py:31
  47.9 14.9 %copy-start.9 = (f32[7]{0:T(128)S(1)}, f32[7]{0:T(128)}, u32[]{:S(2)}) copy-start(f32[7]{0:T(128)} %constant.158.clone) | copy-start | bytes 88
  49.4 7.7 %collective-permute-start = (f32[7,256,12]{1,0,2:T(8,128)S(1)}, f32[7,256,12]{1,0,2:T(8,128)}, u32[]{:S(2)}, u32[]{:S(2)}) collective-permute-start(f32[7,256,12]{1,0,2:T(8,128)S(1)} %copy.37), channel_id=1, source_target_pairs={{0,6},{2,8},{4,10},{6,12},{8,14},{10,16},{12,18},{14,20},{16,22},{... | collective-permute-start | bytes 258056 | tf_op jit(solution)/shard_map/ppermute | solution.py:31
  49.5 9.8 %collective-permute-start.1 = (f32[7,256,12]{1,0,2:T(8,128)S(1)}, f32[7,256,12]{1,0,2:T(8,128)}, u32[]{:S(2)}, u32[]{:S(2)}) collective-permute-start(f32[7,256,12]{1,0,2:T(8,128)S(1)} %copy.37), channel_id=1, source_target_pairs={{0,30},{2,0},{4,2},{6,4},{8,6},{10,8},{12,10},{14,12},{16,14},{18,... | collective-permute-start | bytes 258056 | tf_op jit(solution)/shard_map/ppermute | solution.py:31
  61.5 5.4 %copy-start.13 = (f32[2]{0:T(128)S(1)}, f32[2]{0:T(128)}, u32[]{:S(2)}) copy-start(f32[2]{0:T(128)} %get-tuple-element.59) | copy-start | bytes 28
  62.8 12.8 %copy-start.2 = (f32[2,256,512]{2,1,0:T(8,128)S(1)}, f32[2,256,512]{2,1,0:T(8,128)}, u32[]{:S(2)}) copy-start(f32[2,256,512]{2,1,0:T(8,128)} %get-tuple-element.77) | copy-start | bytes 3145732
  62.8 12.7 %copy-start.4 = (f32[2,256,512]{2,1,0:T(8,128)S(1)}, f32[2,256,512]{2,1,0:T(8,128)}, u32[]{:S(2)}) copy-start(f32[2,256,512]{2,1,0:T(8,128)} %copy-done.3) | copy-start | bytes 3145732
  62.8 12.7 %copy-start.5 = (f32[7,256,12]{2,1,0:T(8,128)S(1)}, f32[7,256,12]{2,1,0:T(8,128)}, u32[]{:S(2)}) copy-start(f32[7,256,12]{2,1,0:T(8,128)} %broadcast_select_fusion.2) | copy-start | bytes 258052
  62.8 12.7 %copy-start.6 = (f32[1,256,512]{2,1,0:T(8,128)S(1)}, f32[1,256,512]{2,1,0:T(8,128)}, u32[]{:S(2)}) copy-start(f32[1,256,512]{2,1,0:T(8,128)} %param.23) | copy-start | bytes 1572868
  64.3 7.0 %collective-permute-start.4 = (f32[7,16,640]{2,1,0:T(8,128)S(1)}, f32[7,16,640]{2,1,0:T(8,128)S(1)}, u32[]{:S(2)}, u32[]{:S(2)}) collective-permute-start(f32[7,16,640]{2,1,0:T(8,128)S(1)} %get-tuple-element.65), channel_id=1, source_target_pairs={{0,8},{2,10},{4,12},{6,14},{8,16},{10,18},{12,20},{14,22},{16,24},... | collective-permute-start | bytes 860168 | tf_op jit(solution)/shard_map/ppermute | solution.py:26
  65.6 9.8 %collective-permute-start.5 = (f32[7,16,640]{2,1,0:T(8,128)S(1)}, f32[7,16,640]{2,1,0:T(8,128)S(1)}, u32[]{:S(2)}, u32[]{:S(2)}) collective-permute-start(f32[7,16,640]{2,1,0:T(8,128)S(1)} %get-tuple-element.66), channel_id=1, source_target_pairs={{8,0},{10,2},{12,4},{14,6},{16,8},{18,10},{20,12},{22,14},{24,16},... | collective-permute-start | bytes 860168 | tf_op jit(solution)/shard_map/ppermute | solution.py:26
  120.6 0.6 copy-start.8
Sparse Core Ops, SparseCore 0:
  10.2 23.9 all-gather.1

commit v3 on v2

--- a/solution.py
+++ b/solution.py
@@ -26,21 +26,23 @@
     return lax.ppermute(block, axis, route)
 
 
-def passed_along_2(array, axis, by):
+def around_row(array, axis, by):
     devices = lax.axis_size(axis)
-    return lax.ppermute(array, axis, [(i, (i + by) % devices) for i in range(devices)])
-
-
-def from_west(edge, column_tile):
-    near = passed_along_2(edge, "space", 1)
-    far = passed_along_2(edge, "space", -(TX - 1))
-    return jnp.where(column_tile == 0, far, near)
-
-
-def from_east(edge, column_tile):
-    near = passed_along_2(edge, "space", -1)
-    far = passed_along_2(edge, "space", TX - 1)
-    return jnp.where(column_tile == TX - 1, far, near)
+    route = [(i, i // TX * TX + (i + by) % TX) for i in range(devices)]
+    return lax.ppermute(array, axis, route)
+
+
+def surrounded(fields, fill, width, rim, row_tile, last_row):
+    fill = jnp.array(fill, jnp.float32)[:, None, None]
+    west = around_row(fields[:, :, -width:], "space", 1)
+    east = around_row(fields[:, :, :width], "space", -1)
+    gap = jnp.broadcast_to(fill, (*fields.shape[:2], LANES - 2 * width))
+    wide = jnp.concatenate([fields, east, gap, west], axis=-1)
+    north = passed_along(wide[:, -rim:, :], "space", TX)
+    south = passed_along(wide[:, :rim, :], "space", -TX)
+    north = jnp.where(row_tile == 0, fill, north)
+    south = jnp.where(row_tile == last_row, fill, south)
+    return jnp.concatenate([north, wide, south], axis=-2)
 
 
 def face(depth_sum, slope):
@@ -238,22 +240,15 @@
         [time_step * 0.5 ** (5.0 / 3.0) / rough, time_step * conduct, time_step * conduct * suction_p]
     )
     group_mean = jnp.mean(prior_weight)
-    column_tile = lax.axis_index("space") % TX
     row_tile = lax.axis_index("space") // TX
     land = land_mask[0] > 0
     forced = lax.all_gather(forcing, "dom", axis=3, tiled=True)[:, :, 0].astype(jnp.float32)
     rain = jnp.where(land[None], time_step * (forced[:, 0] - forced[:, 1]), DRY)
-    fields = jnp.concatenate([water, soaked, terrain, rain], axis=0)
-    fill = jnp.array([0.0] * parts + [1.0] * parts + [0.0] + [DRY] * hours, jnp.float32)[:, None, None]
-    west = from_west(fields[:, :, -width:], column_tile)
-    east = from_east(fields[:, :, :width], column_tile)
-    gap = jnp.broadcast_to(fill, (fields.shape[0], rows, LANES - 2 * width))
-    wide = jnp.concatenate([fields, east, gap, west], axis=-1)
-    north = passed_along(wide[:, -rim:, :], "space", TX)
-    south = passed_along(wide[:, :rim, :], "space", -TX)
-    north = jnp.where(row_tile == 0, fill, north)
-    south = jnp.where(row_tile == n_space // TX - 1, fill, south)
-    big = jnp.concatenate([north, wide, south], axis=-2)
+    fields = jnp.concatenate([water, soaked, terrain], axis=0)
+    fill = [0.0] * parts + [1.0] * parts + [0.0]
+    last_row = n_space // TX - 1
+    big = surrounded(fields, fill, width, rim, row_tile, last_row)
+    rain = surrounded(rain, [DRY] * hours, width, rim, row_tile, last_row)
     high, across = big.shape[1:]
     seen = jnp.where(land[None], observed[:, 0].astype(jnp.float32), -1.0)
     vmem = pl.BlockSpec(memory_space=pltpu.VMEM)
@@ -275,7 +270,7 @@
             pltpu.VMEM((high, across), jnp.float32),
         ],
         compiler_params=pltpu.CompilerParams(vmem_limit_bytes=48 * 2**20),
-    )(params, big[:parts], big[parts : 2 * parts], big[2 * parts], big[2 * parts + 1 :], seen)
+    )(params, big[:parts], big[parts : 2 * parts], big[2 * parts], rain, seen)
     misfit = jnp.sum(missed, axis=(1, 2))
     cells = hours * jnp.sum(land.astype(jnp.float32))
     mine = jnp.zeros((ROWS, LANES), jnp.float32).at[0, :parts].set(misfit).at[1].set(cells).at[2].set(group_mean)

time: 140 us -> 130 us (0.929)
  waiting for transfers between devices: 24 us -> 13.6 us
  starting transfers between devices: 10 us -> 15.7 us
  local copies, waits for them, and re-layouts: 19 us -> 14.2 us
  other arithmetic: 18.5 us -> 16.1 us
    all_gather x1, waiting for transfers between devices: 15.5 us -> 0.01 us  [local(): lax.all_gather(forcing, 'dom', axis=3, tiled=True)[:, :, 0]]
    ppermute x2 -> x4, starting transfers between devices: 2.6 us -> 11.4 us  [passed_along(): return lax.ppermute(block, axis, route)]
    ppermute x4, waiting for transfers between devices: 0.01 us -> 5.71 us  [around_row(): return lax.ppermute(array, axis, route)]
    ppermute x4 -> x2, local copies, waits for them, and re-layouts: 6.87 us -> 3.08 us  [around_row(): return lax.ppermute(array, axis, route)]
    ppermute x4, starting transfers between devices: 7.38 us -> 4.28 us  [around_row(): return lax.ppermute(array, axis, route)]
    select_n x3, other arithmetic: 3.6 us -> 1.05 us  [the longest x2 1.04 us: surrounded(): north = jnp.where(row_tile == 0, fill, north)]
    concatenate x1 -> x2, other arithmetic: 2.34 us -> 4.28 us  [surrounded(): return jnp.concatenate([north, wide, south], axis=-2)]
    slice x2 -> x3, other arithmetic: 4.19 us -> 3.32 us  [the longest x2 2.05 us: surrounded(): north = passed_along(wide[:, -rim:, :], 'space', TX)]
  transfers between devices with their start and end apart: 7 -> 9, of which waited for: 3 -> 5; matrix products, arithmetic and copies ran while one was open for 13% -> 13% of each run, Pallas kernels for 0% -> 0%
where the time goes in v3:
time: 130 us; the launch traced here: 129 us
  Pallas kernels  53.5 us (41%)
  other arithmetic  16.1 us (12%)
  starting transfers between devices  15.7 us (12%)
  between operations  15.6 us (12%)
  local copies, waits for them, and re-layouts  14.2 us (11%)
  waiting for transfers between devices  13.6 us (10%)
    pallas_call x1, Pallas kernels, local(): pl.pallas_call(functools.partial(window_kernel, hours, width, rim), out_s...  42 us
    pallas_call x1, Pallas kernels, local(): pl.pallas_call(functools.partial(weigh_kernel, n_space, n_dom, parts), ou...  11.6 us
    ppermute x4, starting transfers between devices, passed_along(): return lax.ppermute(block, axis, route)  11.4 us
    ppermute x4, waiting for transfers between devices, passed_along(): return lax.ppermute(block, axis, route)  7.89 us
    ppermute x4, waiting for transfers between devices, around_row(): return lax.ppermute(array, axis, route)  5.71 us
    ppermute x4, starting transfers between devices, around_row(): return lax.ppermute(array, axis, route)  4.28 us
    concatenate x2, other arithmetic, surrounded(): return jnp.concatenate([north, wide, south], axis=-2)  4.28 us
    ppermute x2, local copies, waits for them, and re-layouts, around_row(): return lax.ppermute(array, axis, route)  3.08 us
  transfers between devices with their start and end apart: 9, of which 5 were waited for; matrix products, arithmetic and copies ran while one was open for 13% of the time, Pallas kernels for 0%

profile of v3, /device:TPU:0, one launch (start us, length us, event | category | flops | bytes accessed | tf_op | source)
XLA Modules:
  0.0 128.8 jit_solution(13487504053939370130)
XLA Ops:
  7.2 0.0 copy-start
  7.2 0.0 copy-start.5
  7.2 0.0 all-gather.2.cloned.1.call-start
  7.2 0.8 compare_and_fusion
  8.0 0.4 copy-done
  8.4 1.6 %gather_fusion.1 = f32[2,256,512]{2,1,0:T(8,128)} fusion(f32[2,256,512]{2,1,0:T(8,128)S(1)} %bitcast.34, s32[1024]{0:T(1024)S(1)} %pad_clamp_fusion), kind=kCustom, calls=%fused_computation.clone | custom fusion | bytes 2097160 | tf_op jit(solution)/shard_map/jit(_take)/gather | solution.py:229
  10.0 0.0 copy-done.5
  10.0 1.6 %gather_fusion.2 = f32[2,256,512]{2,1,0:T(8,128)} fusion(f32[2,256,512]{2,1,0:T(8,128)S(1)} %bitcast.35, s32[1024]{0:T(1024)S(1)} %pad_clamp_fusion), kind=kCustom, calls=%fused_computation.1.clone | custom fusion | bytes 2097160 | tf_op jit(solution)/shard_map/jit(_take)/gather | solution.py:230
  11.6 2.0 %broadcast_select_fusion.1 = (f32[2,256,512]{2,1,0:T(8,128)S(1)}, f32[2,256,512]{2,1,0:T(8,128)S(1)}) fusion(f32[2,256,512]{2,1,0:T(8,128)} %gather_fusion.1, pred[2]{0:T(512)(128)(4,1)S(1)} %get-tuple-element.63, f32[2,256,512]{2,1,0:T(8,128)} %gather_fusion.2), kind=kLoop, calls=%fused_computation.16 | loop fusion | flops 524288 | bytes 4194306 | tf_op jit(solution)/shard_map/jit(_take)/select_n | solution.py:229
  13.6 0.0 copy-done.4
  13.6 1.3 pad_maximum_fusion.4
  14.9 1.4 %copy.34 = f32[5,256,12]{1,2,0:T(8,128)S(1)} copy(f32[5,256,12]{2,1,0:T(8,128)} %get-tuple-element.70) | data formatting | bytes 122880 | tf_op jit(solution)/shard_map/slice | solution.py:37
  16.2 0.5 collective-permute-start.1
  16.7 1.3 %copy.33 = f32[5,256,12]{1,2,0:T(8,128)S(1)} copy(f32[5,256,12]{2,1,0:T(8,128)} %get-tuple-element.69) | data formatting | bytes 122880 | tf_op jit(solution)/shard_map/slice | solution.py:38
  18.0 2.0 %collective-permute-start = (f32[5,256,12]{1,2,0:T(8,128)S(1)}, f32[5,256,12]{1,2,0:T(8,128)}, u32[]{:S(2)}, u32[]{:S(2)}) collective-permute-start(f32[5,256,12]{1,2,0:T(8,128)S(1)} %copy.33), channel_id=1, source_target_pairs={{0,6},{2,0},{4,2},{6,4},{8,14},{10,8},{12,10},{14,12},{16,22},{18,... | collective-permute-start | bytes 184328 | tf_op jit(solution)/shard_map/ppermute | solution.py:32
  20.0 1.9 %copy.37 = bf16[2,2,1,128,512]{4,3,0,1,2:T(8,128)(2,1)} copy(bf16[2,2,1,128,512]{4,3,2,1,0:T(8,128)(2,1)} %param.26) | data formatting | bytes 1048576 | tf_op args[4]
  21.9 0.0 all-gather.2.cloned.1.call-update
  22.0 0.0 copy-done.1
  22.0 0.6 gather_fusion
  22.6 1.8 %convert_reduce_fusion = (f32[]{:T(128)}, pred[1,256,512]{2,1,0:T(8,128)(4,1)S(1)}) fusion(s32[1,256,512]{2,1,0:T(8,128)} %param.25), kind=kLoop, calls=%fused_computation.17 | loop fusion | flops 393215 | bytes 655364 | tf_op jit(solution)/shard_map/reduce_sum | solution.py:275
  24.4 0.0 copy-done.9
  24.4 0.0 copy-done.10
  24.4 0.0 copy-done.11
  24.4 0.2 select_reduce_fusion.2
  24.6 0.0 collective-permute-done.1
  24.6 1.1 copy.36
  25.7 0.0 collective-permute-done
  25.7 2.0 %copy.35 = f32[5,256,12]{2,1,0:T(8,128)} copy(f32[5,256,12]{1,2,0:T(8,128)} %collective-permute-done) | data formatting | bytes 122880 | tf_op jit(solution)/shard_map/ppermute | solution.py:32
  27.7 0.0 copy-done.8
  27.7 0.1 broadcast_in_dim.113
  27.8 0.0 copy-start.3
  27.9 0.0 copy-start.12
  27.9 2.0 %pad_maximum_fusion.10 = (f32[5,16,640]{2,1,0:T(8,128)}, f32[5,16,640]{2,1,0:T(8,128)}) fusion(f32[5,256,12]{2,1,0:T(8,128)} %copy.36, f32[5,256,104]{2,1,0:T(8,128)S(1)} %broadcast_in_dim.113, f32[5,256,12]{2,1,0:T(8,128)} %copy.35, f32[1,256,512]{2,1,0:T(8,128)} %param.24, f32[2,256,512]{2,1,0:T(8,128)S(1)} %get-tuple-element.80, ...), kind=kLoop, calls=%fused_computation.24 | loop fusion | flops 512000 | bytes 3686400 | tf_op jit(solution)/shard_map/slice | solution.py:41
  29.8 0.0 copy-done.3
  29.8 4.3 %collective-permute-start.2 = (f32[5,16,640]{2,1,0:T(8,128)}, f32[5,16,640]{2,1,0:T(8,128)S(1)}, u32[]{:S(2)}, u32[]{:S(2)}) collective-permute-start(f32[5,16,640]{2,1,0:T(8,128)} %get-tuple-element.65), channel_id=1, source_target_pairs={{0,8},{2,10},{4,12},{6,14},{8,16},{10,18},{12,20},{14,22},{16,24},... | collective-permute-start | bytes 614408 | tf_op jit(solution)/shard_map/ppermute | solution.py:26
  34.1 1.3 %collective-permute-start.3 = (f32[5,16,640]{2,1,0:T(8,128)}, f32[5,16,640]{2,1,0:T(8,128)}, u32[]{:S(2)}, u32[]{:S(2)}) collective-permute-start(f32[5,16,640]{2,1,0:T(8,128)} %get-tuple-element.66), channel_id=1, source_target_pairs={{8,0},{10,2},{12,4},{14,6},{16,8},{18,10},{20,12},{22,14},{24,16},... | collective-permute-start | bytes 614408 | tf_op jit(solution)/shard_map/ppermute | solution.py:26
  36.1 0.0 copy-done.12
  36.1 0.6 reduce_sum.62
  37.4 1.4 %collective-permute-done.2 = f32[5,16,640]{2,1,0:T(8,128)S(1)} collective-permute-done((f32[5,16,640]{2,1,0:T(8,128)}, f32[5,16,640]{2,1,0:T(8,128)S(1)}, u32[]{:S(2)}, u32[]{:S(2)}) %collective-permute-start.2) | collective-permute-done | bytes 204832 | tf_op jit(solution)/shard_map/ppermute | solution.py:26
  38.8 4.1 %collective-permute-done.3 = f32[5,16,640]{2,1,0:T(8,128)} collective-permute-done((f32[5,16,640]{2,1,0:T(8,128)}, f32[5,16,640]{2,1,0:T(8,128)}, u32[]{:S(2)}, u32[]{:S(2)}) %collective-permute-start.3) | collective-permute-done | bytes 204832 | tf_op jit(solution)/shard_map/ppermute | solution.py:26
  42.9 1.0 broadcast_select_fusion.3
  43.9 4.1 %pad_maximum_fusion = f32[5,288,640]{2,1,0:T(8,128)} fusion(f32[5,16,640]{2,1,0:T(8,128)S(1)} %get-tuple-element.78, f32[5,256,12]{2,1,0:T(8,128)} %copy.36, f32[5,256,104]{2,1,0:T(8,128)} %copy-done.3, f32[5,256,12]{2,1,0:T(8,128)} %copy.35, f32[1,256,512]{2,1,0:T(8,128)} %param.24, f32[2,256,512]{2,1,0:T(8,128)S(1)} %get-tuple-element.80, ...), kind=kLoop, calls=%fused_computation.3 | loop fusion | flops 6451200 | bytes 7372800 | tf_op jit(solution)/shard_map/concatenate | solution.py:45
  48.0 1.6 %bitcast_convert_fusion = f32[2,2,256,512]{3,2,0,1:T(8,128)S(1)} fusion(bf16[2,2,1,256,512]{4,3,0,1,2:T(8,128)(2,1)} %all-gather.2.cloned.1.call-done), kind=kLoop, calls=%fused_computation.10 | loop fusion | flops 524288 | bytes 3145728 | tf_op jit(solution)/shard_map/convert_element_type | solution.py:245
  49.6 0.0 copy-done.6
  49.6 0.0 copy-start.2
  49.6 0.4 convert_select_fusion
  50.0 0.1 fusion.4
  50.2 0.1 collective-permute-start.5
  50.2 1.7 %collective-permute-start.4 = (f32[2,256,12]{2,1,0:T(8,128)S(1)}, f32[2,256,12]{2,1,0:T(8,128)S(1)}, u32[]{:S(2)}, u32[]{:S(2)}) collective-permute-start(f32[2,256,12]{2,1,0:T(8,128)S(1)} %get-tuple-element.73), channel_id=1, source_target_pairs={{0,6},{2,0},{4,2},{6,4},{8,14},{10,8},{12,10},{14,12},{16,22},{18,... | collective-permute-start | bytes 73736 | tf_op jit(solution)/shard_map/ppermute | solution.py:32
  52.0 0.0 copy-done.2
  52.0 0.2 fusion.3
  52.2 5.7 %collective-permute-done.5 = f32[2,256,12]{2,1,0:T(8,128)S(1)} collective-permute-done((f32[2,256,12]{2,1,0:T(8,128)S(1)}, f32[2,256,12]{2,1,0:T(8,128)S(1)}, u32[]{:S(2)}, u32[]{:S(2)}) %collective-permute-start.5) | collective-permute-done | bytes 24608 | tf_op jit(solution)/shard_map/ppermute | solution.py:32
  57.9 0.0 collective-permute-done.4
  57.9 0.1 pad_maximum_fusion.14
  58.0 1.3 %collective-permute-start.7 = (f32[2,16,640]{2,1,0:T(8,128)S(1)}, f32[2,16,640]{2,1,0:T(8,128)S(1)}, u32[]{:S(2)}, u32[]{:S(2)}) collective-permute-start(f32[2,16,640]{2,1,0:T(8,128)S(1)} %get-tuple-element.72), channel_id=1, source_target_pairs={{8,0},{10,2},{12,4},{14,6},{16,8},{18,10},{20,12},{22,14},{24,16},... | collective-permute-start | bytes 245768 | tf_op jit(solution)/shard_map/ppermute | solution.py:26
  59.3 4.6 %collective-permute-start.6 = (f32[2,16,640]{2,1,0:T(8,128)S(1)}, f32[2,16,640]{2,1,0:T(8,128)S(1)}, u32[]{:S(2)}, u32[]{:S(2)}) collective-permute-start(f32[2,16,640]{2,1,0:T(8,128)S(1)} %get-tuple-element.71), channel_id=1, source_target_pairs={{0,8},{2,10},{4,12},{6,14},{8,16},{10,18},{12,20},{14,22},{16,24},... | collective-permute-start | bytes 245768 | tf_op jit(solution)/shard_map/ppermute | solution.py:26
  63.9 1.1 collective-permute-done.7
  65.0 1.2 collective-permute-done.6
  66.3 0.2 pad_maximum_fusion.1.r_ref
  66.5 42.0 %shard_map.157 = (f32[2,256,512]{2,1,0:T(8,128)}, f32[2,256,512]{2,1,0:T(8,128)}, f32[2,8,128]{2,1,0:T(8,128)S(1)}) custom-call(f32[3,2]{1,0:T(4,128)S(1)} %pad_maximum_fusion.15.par_ref, f32[2,288,640]{2,1,0:T(8,128)S(1)} %get-tuple-element.68.d_in, f32[2,288,640]{2,1,0:T(8,128)S(1)} %get-tuple-element.67.s_in, f32[288,640]{1,0:T(8,128)S(1)} %slice_bitcast_fusion.g_ref, ...), custom_call_target="tpu_custom_call" | custom-call | tf_op jit(solution)/shard_map/pallas_call | solution.py:255
  108.4 0.1 reduce_sum.60
  108.6 0.6 copy-done.7
  109.2 11.6 %shard_map.158 = f32[8,128]{1,0:T(8,128)} custom-call(f32[8,128]{1,0:T(8,128)} %copy-done.7), custom_call_target="tpu_custom_call" | custom-call | tf_op jit(solution)/shard_map/pallas_call | solution.py:278
  120.8 1.2 slice_bitcast_fusion.1
  (23 shorter events, 0.2 us)
Async XLA Ops:
  7.2 1.2 copy-start
  7.2 2.8 %copy-start.5 = (f32[2,1,256,512]{3,2,1,0:T(8,128)S(1)}, f32[2,1,256,512]{3,2,1,0:T(8,128)}, u32[]{:S(2)}) copy-start(f32[2,1,256,512]{3,2,1,0:T(8,128)} %param.23) | copy-start | bytes 3145732
  7.2 40.8 %all-gather.2.cloned.1.call-start = ((), (), s32[]{:S(2)}) async-start(), calls=%async_computation | async-start | bytes 1572864 | tf_op jit(solution)/shard_map/all_gather | solution.py:245
  11.6 2.0 %copy-start.4 = (f32[1,256,512]{2,1,0:T(8,128)S(1)}, f32[1,256,512]{2,1,0:T(8,128)}, u32[]{:S(2)}) copy-start(f32[1,256,512]{2,1,0:T(8,128)} %param.24) | copy-start | bytes 1572868
  14.9 7.1 %copy-start.1 = (s32[2]{0:T(128)S(1)}, s32[2]{0:T(128)}, u32[]{:S(2)}) copy-start(s32[2]{0:T(128)} %param.31) | copy-start | bytes 28
  14.9 9.5 %copy-start.9 = (f32[4]{0:T(128)S(1)}, f32[4]{0:T(128)}, u32[]{:S(2)}) copy-start(f32[4]{0:T(128)} %param.30) | copy-start | bytes 52
  14.9 9.5 %copy-start.10 = (f32[4]{0:T(128)S(1)}, f32[4]{0:T(128)}, u32[]{:S(2)}) copy-start(f32[4]{0:T(128)} %param.29) | copy-start | bytes 52
  14.9 9.5 %copy-start.11 = (f32[4]{0:T(128)S(1)}, f32[4]{0:T(128)}, u32[]{:S(2)}) copy-start(f32[4]{0:T(128)} %param.28) | copy-start | bytes 52
  16.2 8.4 %collective-permute-start.1 = (f32[5,256,12]{1,2,0:T(8,128)S(1)}, f32[5,256,12]{1,2,0:T(8,128)S(1)}, u32[]{:S(2)}, u32[]{:S(2)}) collective-permute-start(f32[5,256,12]{1,2,0:T(8,128)S(1)} %copy.34), channel_id=1, source_target_pairs={{0,2},{2,4},{4,6},{6,0},{8,10},{10,12},{12,14},{14,8},{16,18},{18,... | collective-permute-start | bytes 184328 | tf_op jit(solution)/shard_map/ppermute | solution.py:32
  18.0 9.7 %copy-start.8 = (f32[5]{0:T(128)S(1)}, f32[5]{0:T(128)}, u32[]{:S(2)}) copy-start(f32[5]{0:T(128)} %constant.150.clone) | copy-start | bytes 64
  18.0 7.7 %collective-permute-start = (f32[5,256,12]{1,2,0:T(8,128)S(1)}, f32[5,256,12]{1,2,0:T(8,128)}, u32[]{:S(2)}, u32[]{:S(2)}) collective-permute-start(f32[5,256,12]{1,2,0:T(8,128)S(1)} %copy.33), channel_id=1, source_target_pairs={{0,6},{2,0},{4,2},{6,4},{8,14},{10,8},{12,10},{14,12},{16,22},{18,... | collective-permute-start | bytes 184328 | tf_op jit(solution)/shard_map/ppermute | solution.py:32
  27.8 2.0 %copy-start.3 = (f32[5,256,104]{2,1,0:T(8,128)}, f32[5,256,104]{2,1,0:T(8,128)S(1)}, u32[]{:S(2)}) copy-start(f32[5,256,104]{2,1,0:T(8,128)S(1)} %broadcast_in_dim.113) | copy-start | bytes 1597444
  27.9 8.2 %copy-start.12 = (f32[2]{0:T(128)S(1)}, f32[2]{0:T(128)}, u32[]{:S(2)}) copy-start(f32[2]{0:T(128)} %param.33) | copy-start | bytes 28
  29.8 9.0 %collective-permute-start.2 = (f32[5,16,640]{2,1,0:T(8,128)}, f32[5,16,640]{2,1,0:T(8,128)S(1)}, u32[]{:S(2)}, u32[]{:S(2)}) collective-permute-start(f32[5,16,640]{2,1,0:T(8,128)} %get-tuple-element.65), channel_id=1, source_target_pairs={{0,8},{2,10},{4,12},{6,14},{8,16},{10,18},{12,20},{14,22},{16,24},... | collective-permute-start | bytes 614408 | tf_op jit(solution)/shard_map/ppermute | solution.py:26
  34.1 8.8 %collective-permute-start.3 = (f32[5,16,640]{2,1,0:T(8,128)}, f32[5,16,640]{2,1,0:T(8,128)}, u32[]{:S(2)}, u32[]{:S(2)}) collective-permute-start(f32[5,16,640]{2,1,0:T(8,128)} %get-tuple-element.66), channel_id=1, source_target_pairs={{8,0},{10,2},{12,4},{14,6},{16,8},{18,10},{20,12},{22,14},{24,16},... | collective-permute-start | bytes 614408 | tf_op jit(solution)/shard_map/ppermute | solution.py:26
  48.0 1.6 %copy-start.6 = (bf16[2,1,256,512]{3,2,1,0:T(8,128)(2,1)S(1)}, bf16[2,1,256,512]{3,2,1,0:T(8,128)(2,1)}, u32[]{:S(2)}) copy-start(bf16[2,1,256,512]{3,2,1,0:T(8,128)(2,1)} %param.27) | copy-start | bytes 1572868
  49.6 2.4 %copy-start.2 = (f32[5,288,640]{2,1,0:T(8,128)S(1)}, f32[5,288,640]{2,1,0:T(8,128)}, u32[]{:S(2)}) copy-start(f32[5,288,640]{2,1,0:T(8,128)} %pad_maximum_fusion) | copy-start | bytes 11059204
  50.2 7.7 %collective-permute-start.5 = (f32[2,256,12]{2,1,0:T(8,128)S(1)}, f32[2,256,12]{2,1,0:T(8,128)S(1)}, u32[]{:S(2)}, u32[]{:S(2)}) collective-permute-start(f32[2,256,12]{2,1,0:T(8,128)S(1)} %get-tuple-element.74), channel_id=1, source_target_pairs={{0,2},{2,4},{4,6},{6,0},{8,10},{10,12},{12,14},{14,8},{16,18},{18,... | collective-permute-start | bytes 73736 | tf_op jit(solution)/shard_map/ppermute | solution.py:32
  50.2 7.6 %collective-permute-start.4 = (f32[2,256,12]{2,1,0:T(8,128)S(1)}, f32[2,256,12]{2,1,0:T(8,128)S(1)}, u32[]{:S(2)}, u32[]{:S(2)}) collective-permute-start(f32[2,256,12]{2,1,0:T(8,128)S(1)} %get-tuple-element.73), channel_id=1, source_target_pairs={{0,6},{2,0},{4,2},{6,4},{8,14},{10,8},{12,10},{14,12},{16,22},{18,... | collective-permute-start | bytes 73736 | tf_op jit(solution)/shard_map/ppermute | solution.py:32
  58.0 7.0 %collective-permute-start.7 = (f32[2,16,640]{2,1,0:T(8,128)S(1)}, f32[2,16,640]{2,1,0:T(8,128)S(1)}, u32[]{:S(2)}, u32[]{:S(2)}) collective-permute-start(f32[2,16,640]{2,1,0:T(8,128)S(1)} %get-tuple-element.72), channel_id=1, source_target_pairs={{8,0},{10,2},{12,4},{14,6},{16,8},{18,10},{20,12},{22,14},{24,16},... | collective-permute-start | bytes 245768 | tf_op jit(solution)/shard_map/ppermute | solution.py:26
  59.3 6.9 %collective-permute-start.6 = (f32[2,16,640]{2,1,0:T(8,128)S(1)}, f32[2,16,640]{2,1,0:T(8,128)S(1)}, u32[]{:S(2)}, u32[]{:S(2)}) collective-permute-start(f32[2,16,640]{2,1,0:T(8,128)S(1)} %get-tuple-element.71), channel_id=1, source_target_pairs={{0,8},{2,10},{4,12},{6,14},{8,16},{10,18},{12,20},{14,22},{16,24},... | collective-permute-start | bytes 245768 | tf_op jit(solution)/shard_map/ppermute | solution.py:26
  108.6 0.6 copy-start.7
Sparse Core Ops, SparseCore 0:
  22.1 23.3 all-gather.1
